TPU v7x, 1024 devices: a whole 4x4x32 slice. The times are simulated.
1024 devices in a mesh: row: 128 (over z, x), col: 8 (over y, core).
Axes of the slice: x: 4, y: 4, z: 32, core: 2. Of those that a mesh axis runs over, the one named last changes fastest.
Arguments:
- stored_matrix: float32 [20480, 20480], P('row', 'col'), may hold values from -30 to 30, as said below
- panel_block: float32 [20480, 256], P('row'), may hold values from -70 to 70
Outputs:
- updated: float32 [20480, 20480], P('row', 'col')
Inputs may be any that keep to these rules, and one draw needn't show every extreme that they name: The matrix S that stored_matrix holds is symmetric.
All inputs are finite; a program needn't handle non-finite values.
Results may differ from a plain program's by a relative error of at most 0.000073.
Values sent between devices are 32-bit elements; how exact they have to be, the bound alone decides.
No kernel may reach another device: no remote copies, remote signals or barrier semaphores. Data moves between devices by JAX's collectives and lax.ppermute only.
A program may use at most 64 MiB of HBM per device.

v0:
```python
import jax
import jax.numpy as jnp
from jax import lax
from jax.sharding import PartitionSpec as P


def left_solve(factor, rhs):
    return lax.linalg.triangular_solve(factor, rhs, left_side=True, lower=True)


def precise_dot(left_operand, right_operand):
    return jnp.dot(
        left_operand,
        right_operand,
        precision=lax.Precision.HIGHEST,
        preferred_element_type=jnp.float32,
    )


def on_device(stored_matrix, panel_block):
    col_count = lax.axis_size("col")
    piece_rows = panel_block.shape[0] // col_count
    col_index = lax.axis_index("col")
    own_piece = lax.dynamic_slice_in_dim(panel_block, col_index * piece_rows, piece_rows, 0)
    gathered = lax.all_gather(own_piece, "row", axis=0, tiled=True)
    partial_value = precise_dot(stored_matrix, gathered)
    image_rows = lax.psum(partial_value, "col")
    gram_term, cross_term = lax.psum(
        (precise_dot(panel_block.T, panel_block), precise_dot(panel_block.T, image_rows)), "row"
    )
    factor = jnp.linalg.cholesky(gram_term)
    basis_rows = left_solve(factor, panel_block.T).T
    reduced = left_solve(factor, image_rows.T).T
    core_term = left_solve(factor, left_solve(factor, cross_term).T).T
    reflector = 2.0 * reduced - 2.0 * precise_dot(basis_rows, core_term)
    own_reflector = lax.dynamic_slice_in_dim(reflector, col_index * piece_rows, piece_rows, 0)
    basis_cols = left_solve(factor, gathered.T).T
    return (
        stored_matrix
        - precise_dot(basis_rows, lax.all_gather(own_reflector, "row", axis=0, tiled=True).T)
        - precise_dot(reflector, basis_cols.T)
    )


def solution(mesh):
    placed = (P("row", "col"), P("row", None))
    return jax.shard_map(
        on_device, mesh=mesh, in_specs=placed, out_specs=P("row", "col"), check_vma=False
    )
```

profile of v0, /device:TPU:1, one launch (start us, length us, event | category | flops | bytes accessed | tf_op | source)
XLA Modules:
  0.0 1222.6 jit_solution(9813701429891962898)
XLA Ops:
  6.5 1.4 dynamic-slice_bitcast_fusion.1
  8.0 263.5 %all-gather.5.cloned.1.call-done = f32[128,20,256]{2,1,0:T(8,128)} async-done(((f32[1,20,256]{2,1,0:T(8,128)}), f32[128,20,256]{2,1,0:T(8,128)}) %all-gather.5.cloned.1.call-update) | async-done | bytes 2621456 | tf_op jit(solution)/shard_map/all_gather | solution.py:25
  271.5 2.7 reshape.97
  274.2 3.9 convolution_bitcast_fusion.1
  278.2 1.4 fusion.36
  279.6 102.8 %all-reduce.5.cloned.1.call-done = f32[160,256]{1,0:T(8,128)} async-done(((f32[160,256]{1,0:T(8,128)}), f32[160,256]{1,0:T(8,128)}) %all-reduce.5.cloned.1.call-update) | async-done | bytes 163856 | tf_op jit(solution)/shard_map/psum | solution.py:27
  382.3 2.3 convolution_bitcast_fusion
  384.9 483.0 %all-reduce.7.cloned.1.call-done = (f32[256,256]{0,1:T(8,128)}, f32[256,256]{0,1:T(8,128)}) async-done(((f32[256,256]{0,1:T(8,128)}, f32[256,256]{0,1:T(8,128)}), (f32[256,256]{0,1:T(8,128)}, f32[256,256]{0,1:T(8,128)})) %all-reduce.7.cloned.1.call-update) | async-done | bytes 524304 | tf_op jit(solution)/shard_map/psum | solution.py:28
  867.9 1.1 copy.8
  869.0 1.0 fusion.9
  870.0 0.7 copy-done.3
  870.7 11.7 cholesky.50
  882.4 9.8 custom-call.20
  892.3 1.0 constant_dynamic-update-slice_fusion
  893.3 1.1 convolution_subtract_fusion.7
  894.4 11.7 cholesky.105
  908.2 5.4 while.9
  909.0 2.0 bitcast_dynamic-update-slice_fusion.2
  911.6 2.0 bitcast_dynamic-update-slice_fusion.2
  913.6 20.5 %custom-call.24 = f32[2,128,128]{1,2,0:T(8,128)S(1)} custom-call(f32[2,128,128]{2,1,0:T(8,128)} %get-tuple-element.43), custom_call_target="InvertDiagBlocksLowerTriangular" | custom-call | tf_op jit(solution)/shard_map/triangular_solve/custom-call.0 | solution.py:8
  934.8 1.1 fusion.15
  935.9 1.2 convolution_subtract_fusion.5
  937.3 1.2 fusion.13
  938.5 1.3 convolution_subtract_fusion.4
  942.3 2.1 copy.11
  944.4 2.7 fusion.3
  947.2 1.3 convolution_subtract_fusion.2
  948.4 2.3 fusion.22
  950.7 253.0 %all-gather.7.cloned.1.call-done = f32[128,20,256]{2,1,0:T(8,128)} async-done(((f32[1,20,256]{2,1,0:T(8,128)}), f32[128,20,256]{2,1,0:T(8,128)}) %all-gather.7.cloned.1.call-update) | async-done | bytes 2621456 | tf_op jit(solution)/shard_map/all_gather | solution.py:40
  1203.8 4.1 reshape.99
  1207.9 5.2 convolution_subtract_fusion.1
  1213.1 3.0 convolution_subtract_fusion
  (39 shorter events, 5.8 us)
Async XLA Ops:
  6.5 265.0 %all-gather.5.cloned.1.call-start = ((), (), s32[]{:S(2)}) async-start(), calls=%async_computation.1 | async-start | bytes 3170304 | tf_op jit(solution)/shard_map/all_gather | solution.py:25
  7.9 374.4 %all-reduce.5.cloned.1.call-start = ((), (), s32[]{:S(2)}) async-start(), calls=%async_computation | async-start | bytes 327680 | tf_op jit(solution)/shard_map/psum | solution.py:27
  274.2 4.0 copy-start.2
  278.1 589.8 %all-reduce.7.cloned.1.call-start = ((), (), s32[]{:S(2)}) async-start(), calls=%async_computation.3 | async-start | bytes 1048576 | tf_op jit(solution)/shard_map/psum | solution.py:28
  384.6 819.1 %all-gather.7.cloned.1.call-start = ((), (), s32[]{:S(2)}) async-start(), calls=%async_computation.2 | async-start | bytes 3170304 | tf_op jit(solution)/shard_map/all_gather | solution.py:40
  870.0 0.7 copy-start.3
  944.4 2.7 copy-start
  1207.9 5.2 copy-start.1
Sparse Core Ops, SparseCore 0:
  11.5 259.9 all-gather.4
  278.2 104.0 all-reduce.4
  386.2 481.6 all-reduce.6
  942.4 261.3 all-gather.6
where the time goes:
time: 1240 us; the launch traced here: 1220 us
  waiting for transfers between devices  1100 us (89%)
  other arithmetic  55.5 us (4%)
  matrix products  31.6 us (3%)
  local copies, waits for them, and re-layouts  18 us (1%)
  between operations  14.6 us (1%)
    psum x1, waiting for transfers between devices, on_device(): lax.psum((precise_dot(panel_block.T, panel_block), precise_dot(panel_bloc...  483 us
    all_gather x1, waiting for transfers between devices, on_device(): gathered = lax.all_gather(own_piece, 'row', axis=0, tiled=True)  264 us
    all_gather x1, waiting for transfers between devices, on_device(): lax.all_gather(own_reflector, 'row', axis=0, tiled=True)  253 us
    psum x1, waiting for transfers between devices, on_device(): image_rows = lax.psum(partial_value, 'col')  103 us
    another operation x6, other arithmetic, on_device(): factor = jnp.linalg.cholesky(gram_term)  34 us
  transfers between devices with their start and end apart: 4, of which 4 were waited for; matrix products, arithmetic and copies ran while one was open for 1% of the time, Pallas kernels for 0%

commit v1 on v0

v1 whole, which is shorter than its diff:
```python
import jax
import jax.numpy as jnp
from jax import lax
from jax.experimental import pallas as pl
from jax.experimental.pallas import tpu as pltpu
from jax.sharding import Mesh, PartitionSpec as P

FINE = 20
BAND = 256
LANES = 128
HALVES = BAND // LANES
PIECE = FINE * HALVES
SLICE = BAND // 8 * HALVES
FAR, NEAR, XS, YS, CORES = 16, 2, 4, 4, 2
GROUPS = NEAR * XS
COLS = YS * CORES
VMEM = pl.BlockSpec(memory_space=pltpu.VMEM)
PARAMS = pltpu.CompilerParams(vmem_limit_bytes=48 * 1024 * 1024)


def precise(left, right, dims):
    return lax.dot_general(
        left, right, (dims, ((), ())), precision=lax.Precision.HIGHEST, preferred_element_type=jnp.float32
    )


def split(value):
    high = value.astype(jnp.bfloat16)
    return high, (value - high.astype(jnp.float32)).astype(jnp.bfloat16)


def three_pass(left, right, dims):
    (lh, ll), (rh, rl) = left, right

    def one(a, b):
        return lax.dot_general(a, b, (dims, ((), ())), preferred_element_type=jnp.float32)

    return (one(lh, rl) + one(ll, rh)) + one(lh, rh)


def stack_halves(value):
    return jnp.concatenate([value[:, i * LANES : (i + 1) * LANES] for i in range(HALVES)], axis=0)


def assemble(pieces, far, base, rows, target):
    for half in range(HALVES):
        lo = base + half * FINE
        target[rows, half * LANES : (half + 1) * LANES] = jnp.concatenate(
            [pieces[g, far, lo : lo + FINE, :] for g in range(GROUPS)], axis=0
        )


def first_kernel(stored, gathered, panel, columns, payload):
    far_rows = GROUPS * FINE

    @pl.loop(0, FAR)
    def _(far):
        assemble(gathered, far, 0, pl.ds(pl.multiple_of(far * far_rows, 8), far_rows), columns)

    wide = far_rows * 4
    image = jnp.zeros((panel.shape[0], BAND), jnp.float32)
    gram = jnp.zeros((BAND, BAND), jnp.float32)
    for i in range(stored.shape[1] // wide):
        part = columns[i * wide : (i + 1) * wide, :]
        image += three_pass(split(stored[:, i * wide : (i + 1) * wide]), split(part), ((1,), (0,)))
        gram += precise(part, part, ((0,), (0,)))
    cross = precise(panel[...], image, ((0,), (0,)))
    eighth = BAND // COLS
    for c in range(COLS):
        payload[c, :PIECE, :] = stack_halves(image[c * FINE : (c + 1) * FINE, :])
        payload[c, PIECE : PIECE + SLICE, :] = stack_halves(gram[c * eighth : (c + 1) * eighth, :])
        payload[c, PIECE + SLICE :, :] = stack_halves(cross[c * eighth : (c + 1) * eighth, :])


def eliminate(block):
    n = block.shape[0]
    row_id = lax.broadcasted_iota(jnp.int32, (n, 1), 0)
    eye = (lax.broadcasted_iota(jnp.int32, (n, n), 0) == lax.broadcasted_iota(jnp.int32, (n, n), 1)).astype(
        jnp.float32
    )
    work = jnp.concatenate([block, eye], axis=1)
    for j in range(0, n, 2):
        row0, row1 = work[j : j + 1, :], work[j + 1 : j + 2, :]
        p, b, d = row0[:, j : j + 1], row0[:, j + 1 : j + 2], row1[:, j + 1 : j + 2]
        inv0 = 1.0 / p
        inv1 = 1.0 / (d - b * (b * inv0))
        row1 = row1 - (b * inv0) * row0
        f0 = jnp.where(row_id > j + 1, work[:, j : j + 1] * inv0, 0.0)
        f1 = jnp.where(row_id > j + 1, (work[:, j + 1 : j + 2] - f0 * b) * inv1, 0.0)
        work = jnp.where(row_id == j + 1, row1, work - f0 * row0 - f1 * row1)
    pivots = jnp.sum(work[:, :n] * eye, axis=1, keepdims=True)
    return work[:, n:], pivots


def invert(gram, work):
    n, size = 64, BAND
    work[:, :size] = gram
    work[:, size:] = (
        lax.broadcasted_iota(jnp.int32, (size, size), 0) == lax.broadcasted_iota(jnp.int32, (size, size), 1)
    ).astype(jnp.float32)
    scaled = []
    for k in range(size // n):
        lo, hi = k * n, (k + 1) * n
        unit, pivots = eliminate(work[lo:hi, lo:hi])
        rows = precise(unit, work[lo:hi, :], ((1,), (0,)))
        work[lo:hi, :] = rows
        over = rows * (1.0 / pivots)
        scaled.append(over[:, size:])
        if hi < size:
            work[hi:, :] = work[hi:, :] - precise(rows[:, hi:size], over, ((0,), (0,)))
    return jnp.concatenate(scaled, axis=0)


def unstack(ref, lo, rows):
    return jnp.concatenate(
        [
            jnp.concatenate([ref[c, lo + h * rows : lo + (h + 1) * rows, :] for h in range(HALVES)], axis=1)
            for c in range(COLS)
        ],
        axis=0,
    )


def second_kernel(panel, small, left, right, work):
    eighth = BAND // COLS
    image = unstack(small, 0, FINE)
    gram = unstack(small, PIECE, eighth)
    cross = unstack(small, PIECE + SLICE, eighth)
    scaled = invert(gram, work)
    unit = work[:, BAND:]

    def by_inverse(value):
        return precise(precise(value, unit, ((1,), (1,))), scaled, ((1,), (0,)))

    first = 2.0 * by_inverse(panel[...])
    left[...] = first
    right[...] = 2.0 * by_inverse(image - precise(first, cross, ((1,), (0,))))


def third_kernel(place, stored, left, right, columns, own, *rest):
    others, (out, pieces, image) = rest[:-3], rest[-3:]
    near, x = place[0], place[1]
    for shift, block in enumerate((own, *others)):
        source = lax.rem(x - shift + XS, XS)
        for flip in range(NEAR):
            group = lax.rem(near + flip, NEAR) * XS + source
            pieces[group] = block[flip]
    far_rows = GROUPS * FINE

    @pl.loop(0, FAR)
    def _(far):
        assemble(pieces, far, 0, pl.ds(pl.multiple_of(far * far_rows, 8), far_rows), image)

    a, b = split(left[...]), split(right[...])
    wide = far_rows * 4
    for i in range(stored.shape[1] // wide):
        at = slice(i * wide, (i + 1) * wide)
        out[:, at] = stored[:, at] - (
            three_pass(a, split(image[at, :]), ((1,), (1,))) + three_pass(b, split(columns[at, :]), ((1,), (1,)))
        )


def on_device(stored, panel):
    f32 = jnp.float32
    rows, width = stored.shape
    col = ("y", "core")
    group = ("near", "x")
    c = lax.axis_index(col)
    own = stack_halves(lax.dynamic_slice_in_dim(panel, c * FINE, FINE, 0))
    far = lax.all_gather(own, "far", axis=0, tiled=True)
    gathered = lax.all_to_all(jnp.broadcast_to(far[None], (GROUPS, *far.shape)), group, 0, 0)
    pieces_shape = (GROUPS, FAR, PIECE, LANES)
    columns, payload = pl.pallas_call(
        first_kernel,
        out_shape=(
            jax.ShapeDtypeStruct((width, BAND), f32),
            jax.ShapeDtypeStruct((COLS, PIECE + 2 * SLICE, LANES), f32),
        ),
        in_specs=[VMEM] * 3,
        out_specs=(VMEM, VMEM),
        compiler_params=PARAMS,
        name="image_and_gram",
    )(stored, gathered.reshape(pieces_shape), panel)
    summed = jnp.sum(lax.all_to_all(payload, col, 0, 0), axis=0)
    image_own, gram_own, cross_own = jnp.split(summed, (PIECE, PIECE + SLICE), axis=0)

    both = lax.all_gather(jnp.concatenate([image_own, cross_own], axis=0), "far", axis=0)
    image_far = both[:, :PIECE, :]
    cross_far = jnp.sum(both[:, PIECE:, :], axis=0)
    swapped = lax.ppermute(image_far, "near", [(0, 1), (1, 0)])
    image_near = jnp.stack([image_far, swapped])
    cross_parts = lax.all_to_all(jnp.broadcast_to(cross_far[None], (GROUPS, *cross_far.shape)), group, 0, 0)
    others = [lax.ppermute(image_near, "x", [(i, (i + d) % XS) for i in range(XS)]) for d in range(1, XS)]
    cross_own = jnp.sum(cross_parts, axis=0)
    small = lax.all_gather(jnp.concatenate([image_own, gram_own, cross_own], axis=0), col, axis=0)
    left, right = pl.pallas_call(
        second_kernel,
        out_shape=(jax.ShapeDtypeStruct((rows, BAND), f32),) * 2,
        in_specs=[VMEM] * 2,
        out_specs=(VMEM, VMEM),
        scratch_shapes=[pltpu.VMEM((BAND, 2 * BAND), f32)],
        compiler_params=PARAMS,
        name="row_factors",
    )(panel, small)
    place = jnp.stack([lax.axis_index("near"), lax.axis_index("x")]).astype(jnp.int32)
    return pl.pallas_call(
        third_kernel,
        out_shape=jax.ShapeDtypeStruct((rows, width), f32),
        in_specs=[pl.BlockSpec(memory_space=pltpu.SMEM)] + [VMEM] * (4 + XS),
        out_specs=VMEM,
        scratch_shapes=[pltpu.VMEM(pieces_shape, f32), pltpu.VMEM((width, BAND), f32)],
        compiler_params=PARAMS,
        name="update",
    )(place, stored, left, right, columns, image_near, *others)


def solution(mesh):
    sizes = (FAR, NEAR, XS, YS, CORES)
    fine_mesh = Mesh(mesh.devices.reshape(sizes), ("far", "near", "x", "y", "core"))
    row, col = ("far", "near", "x"), ("y", "core")
    return jax.shard_map(
        on_device, mesh=fine_mesh, in_specs=(P(row, col), P(row, None)), out_specs=P(row, col), check_vma=False
    )
```

time: 1240 us -> 223 us (0.18); the launches traced: 1220 us -> 222 us
  waiting for transfers between devices: 1100 us -> 4.57 us
  blocking collectives: 0 us -> 153 us
  other arithmetic: 55.5 us -> 1.19 us
  Pallas kernels: 0 us -> 43.7 us
  matrix products: 31.6 us -> 0 us
  starting transfers between devices: 0.31 us -> 16.7 us
  local copies, waits for them, and re-layouts: 18 us -> 3.26 us
  between operations: 14.6 us -> 0.17 us
    psum x2 -> x0, waiting for transfers between devices: 586 us -> none  [the longest x1 483 us: on_device(): lax.psum((precise_dot(panel_block.T, panel_block), precise_dot(panel_bloc...]
    all_gather x2 -> x0, waiting for transfers between devices: 517 us -> none  [the longest x1 264 us: on_device(): gathered = lax.all_gather(own_piece, 'row', axis=0, tiled=True)]
    all_gather x0 -> x3, blocking collectives: none -> 99.7 us  [the longest x1 43 us: on_device(): far = lax.all_gather(own, 'far', axis=0, tiled=True)]
    another operation x10 -> x2, other arithmetic: 54.5 us -> 0.12 us  [the longest x1 0.08 us: on_device(): jnp.stack([lax.axis_index('near'), lax.axis_index('x')]).astype(jnp.int32)]
    all_to_all x0 -> x2, blocking collectives: none -> 53.1 us  [the longest x1 27.6 us: on_device(): lax.all_to_all(jnp.broadcast_to(far[None], (GROUPS, *far.shape)), group,...]
    pallas_call x0 -> x3, Pallas kernels: none -> 43.7 us  [the longest x1 31.3 us: on_device(): pl.pallas_call(second_kernel, out_shape=(jax.ShapeDtypeStruct((rows, BAND...]
    dot_general x6 -> x0, matrix products: 16.2 us -> none  [precise_dot(): jnp.dot(left_operand, right_operand, precision=lax.Precision.HIGHEST, pre...]
    another operation x17 -> x0, matrix products: 15.4 us -> none  [the longest x15 13.3 us: left_solve(): return lax.linalg.triangular_solve(factor, rhs, left_side=True, lower=True)]
  transfers between devices with their start and end apart: 4 -> 5, of which waited for: 4 -> 1; matrix products, arithmetic and copies ran while one was open for 1% -> 1% of each run, Pallas kernels for 0% -> 14%
where the time goes in v1:
time: 223 us; the launch traced here: 222 us
  blocking collectives  153 us (69%)
  Pallas kernels  43.7 us (20%)
  starting transfers between devices  16.7 us (7%)
  waiting for transfers between devices  4.57 us (2%)
  local copies, waits for them, and re-layouts  3.26 us (1%)
    all_gather x1, blocking collectives, on_device(): far = lax.all_gather(own, 'far', axis=0, tiled=True)  43 us
    all_gather x1, blocking collectives, on_device(): lax.all_gather(jnp.concatenate([image_own, cross_own], axis=0), 'far', ax...  34.1 us
    pallas_call x1, Pallas kernels, on_device(): pl.pallas_call(second_kernel, out_shape=(jax.ShapeDtypeStruct((rows, BAND...  31.3 us
    all_to_all x1, blocking collectives, on_device(): lax.all_to_all(jnp.broadcast_to(far[None], (GROUPS, *far.shape)), group,...  27.6 us
    all_to_all x1, blocking collectives, on_device(): summed = jnp.sum(lax.all_to_all(payload, col, 0, 0), axis=0)  25.5 us
    all_gather x1, blocking collectives, on_device(): lax.all_gather(jnp.concatenate([image_own, gram_own, cross_own], axis=0),...  22.6 us
    ppermute x3, starting transfers between devices, on_device(): lax.ppermute(image_near, 'x', [(i, (i + d) % XS) for i in range(XS)])  9.42 us
    pallas_call x1, Pallas kernels, on_device(): pl.pallas_call(third_kernel, out_shape=jax.ShapeDtypeStruct((rows, width)...  6.49 us
  transfers between devices with their start and end apart: 5, of which 1 were waited for; matrix products, arithmetic and copies ran while one was open for 1% of the time, Pallas kernels for 14%

profile of v1, /device:TPU:1, one launch (start us, length us, event | category | flops | bytes accessed | tf_op | source)
XLA Modules:
  0.0 222.4 jit_solution(10258828058015329088)
XLA Ops:
  0.0 0.8 constant_dynamic-slice_fusion
  0.8 43.0 %all_gather.15 = f32[640,128]{1,0:T(8,128)S(1)} all-gather(f32[40,128]{1,0:T(8,128)S(1)} %pad_maximum_fusion.3), channel_id=1, replica_groups=mesh['far'=16,'near'=2,'x'=4,'y'=4,'core'=2] {'far'}, dimensions={0}, use_global_device_ids=true | all-gather | bytes 348160 | tf_op jit(solution)/shard_map/all_gather | solution.py:170
  43.8 0.2 broadcast_in_dim.4
  44.0 0.0 copy-start
  44.0 0.0 copy-start.2
  44.0 27.6 %all_to_all.15 = f32[8,640,128]{2,1,0:T(8,128)} all-to-all(f32[8,640,128]{2,1,0:T(8,128)S(1)} %broadcast_in_dim.4), channel_id=1, replica_groups=mesh['far'=16,'near'=2,'x'=4,'y'=4,'core'=2] {'near','x'}, dimensions={0} | all-to-all | bytes 5242880 | tf_op jit(solution)/shard_map/all_to_all | solution.py:171
  71.6 0.0 copy-done
  71.6 0.0 copy-done.2
  71.6 5.9 %image_and_gram.1 = (f32[2560,256]{1,0:T(8,128)S(1)}, f32[8,168,128]{2,1,0:T(8,128)S(1)}) custom-call(f32[160,2560]{1,0:T(8,128)S(1)} %copy-done, f32[8,16,40,128]{3,2,1,0:T(8,128)} %bitcast.9, f32[160,256]{1,0:T(8,128)S(1)} %copy-done.2), custom_call_target="tpu_custom_call" | custom-call | tf_op jit(solution)/shard_map/image_and_gram/pallas_call | solution.py:173
  77.5 0.0 copy-start.1
  77.5 1.5 copy-done.1
  79.0 25.5 %all_to_all.16 = f32[8,168,128]{2,1,0:T(8,128)S(1)} all-to-all(f32[8,168,128]{2,1,0:T(8,128)S(1)} %get-tuple-element.9), channel_id=1, replica_groups=mesh['far'=16,'near'=2,'x'=4,'y'=4,'core'=2] {'y','core'}, dimensions={0} | all-to-all | bytes 1376256 | tf_op jit(solution)/shard_map/all_to_all | solution.py:184
  104.6 34.1 %all-gather = f32[1664,128]{1,0:T(8,128)S(1)} all-gather(f32[104,128]{1,0:T(8,128)S(1)} %pad_maximum_fusion.2), channel_id=2, replica_groups=mesh['far'=16,'near'=2,'x'=4,'y'=4,'core'=2] {'far'}, dimensions={0}, use_global_device_ids=true | all-gather | bytes 905216 | tf_op jit(solution)/shard_map/all_gather | solution.py:187
  138.8 0.7 broadcast_in_dim.5
  139.5 4.1 %all-to-all-start.2 = ((f32[8,64,128]{2,1,0:T(8,128)}), f32[8,64,128]{2,1,0:T(8,128)}, u32[]{:S(2)}, u32[]{:S(2)}) async-start(f32[8,64,128]{2,1,0:T(8,128)} %broadcast_in_dim.5), calls=%async_computation.2 | async-start | bytes 524288 | tf_op jit(solution)/shard_map/all_to_all | solution.py:192
  143.6 3.3 %collective-permute-start = (f32[16,40,128]{2,1,0:T(8,128)S(1)}, f32[16,40,128]{2,1,0:T(8,128)S(1)}, u32[]{:S(2)}, u32[]{:S(2)}) collective-permute-start(f32[16,40,128]{2,1,0:T(8,128)S(1)} %get-tuple-element.14), channel_id=1, source_target_pairs={{0,32},{32,0},{1,33},{33,1},{2,34},{34,2},{3,35},{35,3},{4,36},{36... | collective-permute-start | bytes 983048 | tf_op jit(solution)/shard_map/ppermute | solution.py:190
  146.9 4.6 %collective-permute-done = f32[16,40,128]{2,1,0:T(8,128)S(1)} collective-permute-done((f32[16,40,128]{2,1,0:T(8,128)S(1)}, f32[16,40,128]{2,1,0:T(8,128)S(1)}, u32[]{:S(2)}, u32[]{:S(2)}) %collective-permute-start) | collective-permute-done | bytes 327712 | tf_op jit(solution)/shard_map/ppermute | solution.py:190
  151.5 4.5 %collective-permute-start.3 = (f32[2,16,40,128]{3,2,1,0:T(8,128)S(1)}, f32[2,16,40,128]{3,2,1,0:T(8,128)S(1)}, u32[]{:S(2)}, u32[]{:S(2)}) collective-permute-start(f32[2,16,40,128]{3,2,1,0:T(8,128)S(1)} %pad_maximum_fusion.own), channel_id=1, source_target_pairs={{0,24},{8,0},{16,8},{24,16},{1,25},{9,1},{17,9},{25,17},{2,26},{10... | collective-permute-start | bytes 1966088 | tf_op jit(solution)/shard_map/ppermute | solution.py:193
  155.9 2.5 %collective-permute-start.2 = (f32[2,16,40,128]{3,2,1,0:T(8,128)S(1)}, f32[2,16,40,128]{3,2,1,0:T(8,128)}, u32[]{:S(2)}, u32[]{:S(2)}) collective-permute-start(f32[2,16,40,128]{3,2,1,0:T(8,128)S(1)} %pad_maximum_fusion.own), channel_id=1, source_target_pairs={{0,16},{8,24},{16,0},{24,8},{1,17},{9,25},{17,1},{25,9},{2,18},{10... | collective-permute-start | bytes 1966088 | tf_op jit(solution)/shard_map/ppermute | solution.py:193
  158.4 2.5 %collective-permute-start.1 = (f32[2,16,40,128]{3,2,1,0:T(8,128)S(1)}, f32[2,16,40,128]{3,2,1,0:T(8,128)}, u32[]{:S(2)}, u32[]{:S(2)}) collective-permute-start(f32[2,16,40,128]{3,2,1,0:T(8,128)S(1)} %pad_maximum_fusion.own), channel_id=1, source_target_pairs={{0,8},{8,16},{16,24},{24,0},{1,9},{9,17},{17,25},{25,1},{2,10},{10... | collective-permute-start | bytes 1966088 | tf_op jit(solution)/shard_map/ppermute | solution.py:193
  160.9 0.1 pad_add_fusion.place
  161.0 0.0 all-to-all-done.2
  161.0 1.0 reduce_sum.29
  162.0 22.6 %all-gather.1 = f32[1344,128]{1,0:T(8,128)S(1)} all-gather(f32[168,128]{1,0:T(8,128)S(1)} %pad_maximum_fusion.1), channel_id=3, replica_groups=mesh['far'=16,'near'=2,'x'=4,'y'=4,'core'=2] {'y','core'}, dimensions={0}, use_global_device_ids=true | all-gather | bytes 774144 | tf_op jit(solution)/shard_map/all_gather | solution.py:195
  184.6 31.3 %row_factors.1 = (f32[160,256]{1,0:T(8,128)S(1)}, f32[160,256]{1,0:T(8,128)S(1)}) custom-call(f32[160,256]{1,0:T(8,128)S(1)} %copy-done.2, f32[8,168,128]{2,1,0:T(8,128)S(1)} %bitcast.8), custom_call_target="tpu_custom_call" | custom-call | tf_op jit(solution)/shard_map/row_factors/pallas_call | solution.py:196
  215.9 0.0 collective-permute-done.3.rest_2_
  215.9 0.0 collective-permute-done.2.rest_1_
  215.9 0.0 collective-permute-done.1.rest_0_
  215.9 6.5 %update.1 = f32[160,2560]{1,0:T(8,128)} custom-call(s32[2]{0:T(128)S(1)} %pad_add_fusion.place, f32[160,2560]{1,0:T(8,128)S(1)} %copy-done, f32[160,256]{1,0:T(8,128)S(1)} %get-tuple-element.10.left, f32[160,256]{1,0:T(8,128)S(1)} %get-tuple-element.11.right, f32[2560,256]{1,0:T(8,128)} %copy-done.1, f32[2,16,40,128]{3,2,1,0:T(8,128)S(1)} %pad_maximum_fusion.own, ...), custom_call_target="tpu_custom_call" | custom-call | tf_op jit(solution)/shard_map/update/pallas_call | solution.py:206
  (10 shorter events, 0.2 us)
Async XLA Ops:
  44.0 27.6 %copy-start = (f32[160,2560]{1,0:T(8,128)S(1)}, f32[160,2560]{1,0:T(8,128)}, u32[]{:S(2)}) copy-start(f32[160,2560]{1,0:T(8,128)} %stored.3) | copy-start | bytes 4915204
  44.0 27.6 %copy-start.2 = (f32[160,256]{1,0:T(8,128)S(1)}, f32[160,256]{1,0:T(8,128)}, u32[]{:S(2)}) copy-start(f32[160,256]{1,0:T(8,128)} %panel.3) | copy-start | bytes 491524
  77.5 1.5 copy-start.1
  139.5 21.5 %all-to-all-start.2 = ((f32[8,64,128]{2,1,0:T(8,128)}), f32[8,64,128]{2,1,0:T(8,128)}, u32[]{:S(2)}, u32[]{:S(2)}) async-start(f32[8,64,128]{2,1,0:T(8,128)} %broadcast_in_dim.5), calls=%async_computation.2 | async-start | bytes 524288 | tf_op jit(solution)/shard_map/all_to_all | solution.py:192
  143.6 7.8 %collective-permute-start = (f32[16,40,128]{2,1,0:T(8,128)S(1)}, f32[16,40,128]{2,1,0:T(8,128)S(1)}, u32[]{:S(2)}, u32[]{:S(2)}) collective-permute-start(f32[16,40,128]{2,1,0:T(8,128)S(1)} %get-tuple-element.14), channel_id=1, source_target_pairs={{0,32},{32,0},{1,33},{33,1},{2,34},{34,2},{3,35},{35,3},{4,36},{36... | collective-permute-start | bytes 983048 | tf_op jit(solution)/shard_map/ppermute | solution.py:190
  151.5 64.4 %collective-permute-start.3 = (f32[2,16,40,128]{3,2,1,0:T(8,128)S(1)}, f32[2,16,40,128]{3,2,1,0:T(8,128)S(1)}, u32[]{:S(2)}, u32[]{:S(2)}) collective-permute-start(f32[2,16,40,128]{3,2,1,0:T(8,128)S(1)} %pad_maximum_fusion.own), channel_id=1, source_target_pairs={{0,24},{8,0},{16,8},{24,16},{1,25},{9,1},{17,9},{25,17},{2,26},{10... | collective-permute-start | bytes 1966088 | tf_op jit(solution)/shard_map/ppermute | solution.py:193
  155.9 60.0 %collective-permute-start.2 = (f32[2,16,40,128]{3,2,1,0:T(8,128)S(1)}, f32[2,16,40,128]{3,2,1,0:T(8,128)}, u32[]{:S(2)}, u32[]{:S(2)}) collective-permute-start(f32[2,16,40,128]{3,2,1,0:T(8,128)S(1)} %pad_maximum_fusion.own), channel_id=1, source_target_pairs={{0,16},{8,24},{16,0},{24,8},{1,17},{9,25},{17,1},{25,9},{2,18},{10... | collective-permute-start | bytes 1966088 | tf_op jit(solution)/shard_map/ppermute | solution.py:193
  158.4 57.5 %collective-permute-start.1 = (f32[2,16,40,128]{3,2,1,0:T(8,128)S(1)}, f32[2,16,40,128]{3,2,1,0:T(8,128)}, u32[]{:S(2)}, u32[]{:S(2)}) collective-permute-start(f32[2,16,40,128]{3,2,1,0:T(8,128)S(1)} %pad_maximum_fusion.own), channel_id=1, source_target_pairs={{0,8},{8,16},{16,24},{24,0},{1,9},{9,17},{17,25},{25,1},{2,10},{10... | collective-permute-start | bytes 1966088 | tf_op jit(solution)/shard_map/ppermute | solution.py:193

commit v2 on v1

v2 whole, which is shorter than its diff:
```python
import jax
import jax.numpy as jnp
from jax import lax
from jax.experimental import pallas as pl
from jax.experimental.pallas import tpu as pltpu
from jax.sharding import Mesh, PartitionSpec as P

FINE = 20
BAND = 256
LANES = 128
HALVES = BAND // LANES
TILE = 8
PIECE = FINE * HALVES
SLICE = BAND // 8 * HALVES
FAR, NEAR, XS, YS, CORES = 16, 2, 4, 4, 2
GROUPS = NEAR * XS
COLS = YS * CORES
VMEM = pl.BlockSpec(memory_space=pltpu.VMEM)
PARAMS = pltpu.CompilerParams(vmem_limit_bytes=48 * 1024 * 1024)


def precise(left, right, dims):
    return lax.dot_general(
        left, right, (dims, ((), ())), precision=lax.Precision.HIGHEST, preferred_element_type=jnp.float32
    )


def identity(n):
    return (lax.broadcasted_iota(jnp.int32, (n, n), 0) == lax.broadcasted_iota(jnp.int32, (n, n), 1)).astype(
        jnp.float32
    )


def split(value):
    high = value.astype(jnp.bfloat16)
    return high, (value - high.astype(jnp.float32)).astype(jnp.bfloat16)


def three_pass(left, right, dims):
    (lh, ll), (rh, rl) = left, right

    def one(a, b):
        return lax.dot_general(a, b, (dims, ((), ())), preferred_element_type=jnp.float32)

    return (one(lh, rl) + one(ll, rh)) + one(lh, rh)


def stack_halves(value):
    return jnp.concatenate([value[:, i * LANES : (i + 1) * LANES] for i in range(HALVES)], axis=0)


def assemble(pieces, far, base, rows, target):
    for half in range(HALVES):
        lo = base + half * FINE
        target[rows, half * LANES : (half + 1) * LANES] = jnp.concatenate(
            [pieces[g, far, lo : lo + FINE, :] for g in range(GROUPS)], axis=0
        )


def first_kernel(stored, gathered, panel, columns, payload):
    far_rows = GROUPS * FINE

    @pl.loop(0, FAR)
    def _(far):
        assemble(gathered, far, 0, pl.ds(pl.multiple_of(far * far_rows, 8), far_rows), columns)

    wide = far_rows * 4
    image = jnp.zeros((panel.shape[0], BAND), jnp.float32)
    gram = jnp.zeros((BAND, BAND), jnp.float32)
    for i in range(stored.shape[1] // wide):
        part = columns[i * wide : (i + 1) * wide, :]
        image += three_pass(split(stored[:, i * wide : (i + 1) * wide]), split(part), ((1,), (0,)))
        gram += precise(part, part, ((0,), (0,)))
    cross = precise(panel[...], image, ((0,), (0,)))
    eighth = BAND // COLS
    for c in range(COLS):
        payload[c, :PIECE, :] = stack_halves(image[c * FINE : (c + 1) * FINE, :])
        payload[c, PIECE : PIECE + SLICE, :] = stack_halves(gram[c * eighth : (c + 1) * eighth, :])
        payload[c, PIECE + SLICE :, :] = stack_halves(cross[c * eighth : (c + 1) * eighth, :])


def eliminate(block):
    n, wide = block.shape[0], 2 * block.shape[0]
    eye = identity(n)
    work = jnp.concatenate([block, eye], axis=1)
    tiles = [work[i : i + TILE, :] for i in range(0, n, TILE)]
    sub = lax.broadcasted_iota(jnp.int32, (TILE, wide), 0)
    for t in range(n // TILE):
        j = t * TILE
        rows = [tiles[t][k : k + 1, :] for k in range(TILE)]
        square = [
            [jnp.broadcast_to(rows[k][:, j + l : j + l + 1], (1, wide)) if l >= k else None for l in range(TILE)]
            for k in range(TILE)
        ]
        cols = [[jnp.broadcast_to(tile[:, j + k : j + k + 1], (TILE, wide)) for tile in tiles[t:]] for k in range(TILE)]
        for k in range(TILE):
            inverse = 1.0 / square[k][k]
            for m in range(k + 1, TILE):
                factor = square[k][m] * inverse
                rows[m] = rows[m] - factor * rows[k]
                for l in range(m, TILE):
                    square[m][l] = square[m][l] - factor * square[k][l]
            factors = [col * inverse for col in cols[k]]
            factors[0] = jnp.where(sub > k, factors[0], 0.0)
            for l in range(k + 1, TILE):
                cols[l] = [col - f * square[k][l] for col, f in zip(cols[l], factors)]
            for i, f in enumerate(factors):
                tiles[t + i] = tiles[t + i] - f * rows[k]
    work = jnp.concatenate(tiles, axis=0)
    return work[:, n:], jnp.sum(work[:, :n] * eye, axis=1, keepdims=True)


def invert(gram, work, scaled):
    n, size = 64, BAND
    work[:, :size] = gram
    work[:, size:] = identity(size)
    for k in range(size // n):
        lo, hi = k * n, (k + 1) * n
        unit, pivots = eliminate(work[lo:hi, lo:hi])
        rows = precise(unit, work[lo:hi, lo : size + hi], ((1,), (0,)))
        work[lo:hi, lo : size + hi] = rows
        over = rows * (1.0 / pivots)
        scaled[lo:hi, :] = jnp.zeros((n, size), jnp.float32)
        scaled[lo:hi, :hi] = over[:, size - lo :]
        if hi < size:
            work[hi:, hi : size + hi] = work[hi:, hi : size + hi] - precise(
                rows[:, n : size - lo], over[:, n:], ((0,), (0,))
            )


def unstack(ref, lo, rows):
    return jnp.concatenate(
        [
            jnp.concatenate([ref[c, lo + h * rows : lo + (h + 1) * rows, :] for h in range(HALVES)], axis=1)
            for c in range(COLS)
        ],
        axis=0,
    )


def by_inverse(value, unit, scaled):
    return precise(precise(value, unit, ((1,), (1,))), scaled, ((1,), (0,)))


def second_kernel(panel, small, unit, scaled, left, work):
    invert(unstack(small, PIECE, BAND // COLS), work, scaled)
    unit[...] = work[:, BAND:]
    left[...] = 2.0 * by_inverse(panel[...], unit[...], scaled[...])


def third_kernel(stored, left, unit, scaled, small, columns, pieces, out, image):
    far_rows = GROUPS * FINE

    @pl.loop(0, FAR)
    def _(far):
        assemble(pieces, far, 0, pl.ds(pl.multiple_of(far * far_rows, 8), far_rows), image)

    cross = unstack(small, PIECE + SLICE, BAND // COLS)
    own = unstack(small, 0, FINE) - precise(left[...], cross, ((1,), (0,)))
    a, b = split(left[...]), split(2.0 * by_inverse(own, unit[...], scaled[...]))
    wide = far_rows * 4
    for i in range(stored.shape[1] // wide):
        at = slice(i * wide, (i + 1) * wide)
        out[:, at] = stored[:, at] - (
            three_pass(a, split(image[at, :]), ((1,), (1,))) + three_pass(b, split(columns[at, :]), ((1,), (1,)))
        )


def spread(value, axes, count):
    return lax.all_to_all(jnp.broadcast_to(value[None], (count, *value.shape)), axes, 0, 0)


def on_device(stored, panel):
    f32 = jnp.float32
    rows, width = stored.shape
    col = ("y", "core")
    group = ("near", "x")
    c = lax.axis_index(col)
    pieces_shape = (GROUPS, FAR, PIECE, LANES)
    own = stack_halves(lax.dynamic_slice_in_dim(panel, c * FINE, FINE, 0))
    gathered = spread(lax.all_gather(own, "far", axis=0), group, GROUPS)
    columns, payload = pl.pallas_call(
        first_kernel,
        out_shape=(
            jax.ShapeDtypeStruct((width, BAND), f32),
            jax.ShapeDtypeStruct((COLS, PIECE + 2 * SLICE, LANES), f32),
        ),
        in_specs=[VMEM] * 3,
        out_specs=(VMEM, VMEM),
        compiler_params=PARAMS,
        name="image_and_gram",
    )(stored, gathered, panel)
    summed = jnp.sum(lax.all_to_all(payload, col, 0, 0), axis=0)
    far = lax.all_gather(jnp.concatenate([summed[:PIECE], summed[PIECE + SLICE :]], axis=0), "far", axis=0)
    parts = spread(jnp.sum(far[:, PIECE:, :], axis=0), group, GROUPS)
    image_far, parts = lax.optimization_barrier((far[:, :PIECE, :], parts))
    image = spread(image_far, group, GROUPS)
    small = lax.all_gather(
        jnp.concatenate([summed[: PIECE + SLICE], jnp.sum(parts, axis=0)], axis=0), col, axis=0
    )
    square = jax.ShapeDtypeStruct((BAND, BAND), f32)
    unit, scaled, left = pl.pallas_call(
        second_kernel,
        out_shape=(square, square, jax.ShapeDtypeStruct((rows, BAND), f32)),
        in_specs=[VMEM] * 2,
        out_specs=(VMEM,) * 3,
        scratch_shapes=[pltpu.VMEM((BAND, 2 * BAND), f32)],
        compiler_params=PARAMS,
        cost_estimate=pl.CostEstimate(flops=10**10, bytes_accessed=2 * 10**6, transcendentals=0),
        name="factorization",
    )(panel, small)
    return pl.pallas_call(
        third_kernel,
        out_shape=jax.ShapeDtypeStruct((rows, width), f32),
        in_specs=[VMEM] * 7,
        out_specs=VMEM,
        scratch_shapes=[pltpu.VMEM((width, BAND), f32)],
        compiler_params=PARAMS,
        name="update",
    )(stored, left, unit, scaled, small, columns, image)


def solution(mesh):
    sizes = (FAR, NEAR, XS, YS, CORES)
    fine_mesh = Mesh(mesh.devices.reshape(sizes), ("far", "near", "x", "y", "core"))
    row, col = ("far", "near", "x"), ("y", "core")
    return jax.shard_map(
        on_device, mesh=fine_mesh, in_specs=(P(row, col), P(row, None)), out_specs=P(row, col), check_vma=False
    )
```

time: 223 us -> 196 us (0.88)
  Pallas kernels: 43.7 us -> 23 us
  starting transfers between devices: 16.7 us -> 7.81 us
  local copies, waits for them, and re-layouts: 3.26 us -> 6.66 us
    pallas_call x1, Pallas kernels: 31.3 us -> 10.4 us  [on_device(): pl.pallas_call(second_kernel, out_shape=(square, square, jax.ShapeDtypeSt...]
    ppermute x4 -> x0, starting transfers between devices: 12.7 us -> none  [the longest x3 9.42 us: on_device(): lax.ppermute(image_near, 'x', [(i, (i + d) % XS) for i in range(XS)])]
    all_to_all x1 -> x2, waiting for transfers between devices: 0.01 us -> 5.98 us  [spread(): lax.all_to_all(jnp.broadcast_to(value[None], (count, *value.shape)), axes...]
    ppermute x4 -> x0, waiting for transfers between devices: 4.56 us -> none  [the longest x1 4.56 us: on_device(): swapped = lax.ppermute(image_far, 'near', [(0, 1), (1, 0)])]
    all_to_all x1 -> x2, starting transfers between devices: 4.05 us -> 7.81 us  [spread(): lax.all_to_all(jnp.broadcast_to(value[None], (count, *value.shape)), axes...]
  transfers between devices with their start and end apart: 5 -> 2, of which waited for: 1 -> 1; matrix products, arithmetic and copies ran while one was open for 1% -> 0% of each run, Pallas kernels for 14% -> 5%
where the time goes in v2:
time: 196 us; the launch traced here: 195 us
  blocking collectives  152 us (78%)
  Pallas kernels  23 us (12%)
  starting transfers between devices  7.81 us (4%)
  local copies, waits for them, and re-layouts  6.66 us (3%)
  waiting for transfers between devices  5.98 us (3%)
    all_gather x1, blocking collectives, on_device(): gathered = spread(lax.all_gather(own, 'far', axis=0), group, GROUPS)  43 us
    all_gather x1, blocking collectives, on_device(): lax.all_gather(jnp.concatenate([summed[:PIECE], summed[PIECE + SLICE:]],...  34.1 us
    all_to_all x1, blocking collectives, spread(): lax.all_to_all(jnp.broadcast_to(value[None], (count, *value.shape)), axes...  27.6 us
    all_to_all x1, blocking collectives, on_device(): summed = jnp.sum(lax.all_to_all(payload, col, 0, 0), axis=0)  25.5 us
    all_gather x1, blocking collectives, on_device(): lax.all_gather(jnp.concatenate([summed[:PIECE + SLICE], jnp.sum(parts, ax...  21.5 us
    pallas_call x1, Pallas kernels, on_device(): pl.pallas_call(second_kernel, out_shape=(square, square, jax.ShapeDtypeSt...  10.4 us
    all_to_all x2, starting transfers between devices, spread(): lax.all_to_all(jnp.broadcast_to(value[None], (count, *value.shape)), axes...  7.81 us
    pallas_call x1, Pallas kernels, on_device(): pl.pallas_call(third_kernel, out_shape=jax.ShapeDtypeStruct((rows, width)...  6.73 us
  transfers between devices with their start and end apart: 2, of which 1 were waited for; matrix products, arithmetic and copies ran while one was open for 0% of the time, Pallas kernels for 5%

profile of v2, /device:TPU:1, one launch (start us, length us, event | category | flops | bytes accessed | tf_op | source)
XLA Modules:
  0.0 195.4 jit_solution(8250434043709338955)
XLA Ops:
  0.0 0.8 constant_dynamic-slice_fusion
  0.8 43.0 %all-gather = f32[640,128]{1,0:T(8,128)S(1)} all-gather(f32[40,128]{1,0:T(8,128)S(1)} %pad_maximum_fusion.2), channel_id=2, replica_groups=mesh['far'=16,'near'=2,'x'=4,'y'=4,'core'=2] {'far'}, dimensions={0}, use_global_device_ids=true | all-gather | bytes 348160 | tf_op jit(solution)/shard_map/all_gather | solution.py:181
  43.8 0.2 broadcast_in_dim.6
  44.0 0.0 copy-start
  44.0 0.0 copy-start.3
  44.0 27.6 %all_to_all.20.gathered = f32[8,16,40,128]{3,2,1,0:T(8,128)} all-to-all(f32[8,16,40,128]{3,2,1,0:T(8,128)S(1)} %broadcast_in_dim.6), channel_id=1, replica_groups=mesh['far'=16,'near'=2,'x'=4,'y'=4,'core'=2] {'near','x'}, dimensions={0} | all-to-all | bytes 5242880 | tf_op jit(solution)/shard_map/all_to_all | solution.py:170
  71.6 0.0 copy-done
  71.6 0.0 copy-done.3
  71.6 5.9 %image_and_gram.1 = (f32[2560,256]{1,0:T(8,128)S(1)}, f32[8,168,128]{2,1,0:T(8,128)S(1)}) custom-call(f32[160,2560]{1,0:T(8,128)S(1)} %copy-done, f32[8,16,40,128]{3,2,1,0:T(8,128)} %all_to_all.20.gathered, f32[160,256]{1,0:T(8,128)S(1)} %copy-done.3), custom_call_target="tpu_custom_call" | custom-call | tf_op jit(solution)/shard_map/image_and_gram/pallas_call | solution.py:182
  77.5 0.0 copy-start.1
  77.5 1.5 copy-done.1
  79.0 25.5 %all_to_all.21 = f32[8,168,128]{2,1,0:T(8,128)S(1)} all-to-all(f32[8,168,128]{2,1,0:T(8,128)S(1)} %get-tuple-element.12), channel_id=1, replica_groups=mesh['far'=16,'near'=2,'x'=4,'y'=4,'core'=2] {'y','core'}, dimensions={0} | all-to-all | bytes 1376256 | tf_op jit(solution)/shard_map/all_to_all | solution.py:193
  104.6 34.1 %all-gather.1 = f32[1664,128]{1,0:T(8,128)S(1)} all-gather(f32[104,128]{1,0:T(8,128)S(1)} %pad_maximum_fusion.1), channel_id=3, replica_groups=mesh['far'=16,'near'=2,'x'=4,'y'=4,'core'=2] {'far'}, dimensions={0}, use_global_device_ids=true | all-gather | bytes 905216 | tf_op jit(solution)/shard_map/all_gather | solution.py:194
  138.8 0.7 broadcast_in_dim.7
  139.5 3.4 %all-to-all-start.2 = ((f32[8,64,128]{2,1,0:T(8,128)}), f32[8,64,128]{2,1,0:T(8,128)S(1)}, u32[]{:S(2)}, u32[]{:S(2)}) async-start(f32[8,64,128]{2,1,0:T(8,128)} %broadcast_in_dim.7), calls=%async_computation.2 | async-start | bytes 524288 | tf_op jit(solution)/shard_map/all_to_all | solution.py:170
  143.0 6.0 %all-to-all-done.2 = f32[8,64,128]{2,1,0:T(8,128)S(1)} async-done(((f32[8,64,128]{2,1,0:T(8,128)}), f32[8,64,128]{2,1,0:T(8,128)S(1)}, u32[]{:S(2)}, u32[]{:S(2)}) %all-to-all-start.2) | async-done | bytes 262176 | tf_op jit(solution)/shard_map/all_to_all | solution.py:170
  148.9 1.7 broadcast_in_dim.8
  150.6 4.4 %all-to-all-start.3 = ((f32[8,16,40,128]{3,2,1,0:T(8,128)}), f32[8,16,40,128]{3,2,1,0:T(8,128)}, u32[]{:S(2)}, u32[]{:S(2)}) async-start(f32[8,16,40,128]{3,2,1,0:T(8,128)} %broadcast_in_dim.8), calls=%async_computation.3 | async-start | bytes 5242880 | tf_op jit(solution)/shard_map/all_to_all | solution.py:170
  155.1 21.5 %all-gather.2 = f32[1344,128]{1,0:T(8,128)S(1)} all-gather(f32[168,128]{1,0:T(8,128)S(1)} %pad_maximum_fusion), channel_id=4, replica_groups=mesh['far'=16,'near'=2,'x'=4,'y'=4,'core'=2] {'y','core'}, dimensions={0}, use_global_device_ids=true | all-gather | bytes 774144 | tf_op jit(solution)/shard_map/all_gather | solution.py:198
  176.5 10.4 %factorization.1 = (f32[256,256]{1,0:T(8,128)S(1)}, f32[256,256]{1,0:T(8,128)S(1)}, f32[160,256]{1,0:T(8,128)S(1)}) custom-call(f32[160,256]{1,0:T(8,128)S(1)} %copy-done.3, f32[8,168,128]{2,1,0:T(8,128)S(1)} %bitcast.3), custom_call_target="tpu_custom_call" | custom-call | flops 10000000000 | bytes 2000000 | tf_op jit(solution)/shard_map/factorization/pallas_call | solution.py:202
  186.9 0.0 all-to-all-done.3.pieces
  186.9 0.0 copy-start.2
  187.0 1.7 copy-done.2
  188.7 6.7 %update.1 = f32[160,2560]{1,0:T(8,128)} custom-call(f32[160,2560]{1,0:T(8,128)S(1)} %copy-done, f32[160,256]{1,0:T(8,128)S(1)} %get-tuple-element.14.left, f32[256,256]{1,0:T(8,128)S(1)} %get-tuple-element.15.unit, f32[256,256]{1,0:T(8,128)S(1)} %get-tuple-element.16.scaled, f32[8,168,128]{2,1,0:T(8,128)S(1)} %bitcast.4, f32[2560,256]{1,0:T(8,128)S(1)} %copy-done.2, ...), custom_call_target="tpu_custom_call" | custom-call | tf_op jit(solution)/shard_map/update/pallas_call | solution.py:212
  (10 shorter events, 0.1 us)
Async XLA Ops:
  44.0 27.6 %copy-start = (f32[160,2560]{1,0:T(8,128)S(1)}, f32[160,2560]{1,0:T(8,128)}, u32[]{:S(2)}) copy-start(f32[160,2560]{1,0:T(8,128)} %stored.3) | copy-start | bytes 4915204
  44.0 27.6 %copy-start.3 = (f32[160,256]{1,0:T(8,128)S(1)}, f32[160,256]{1,0:T(8,128)}, u32[]{:S(2)}) copy-start(f32[160,256]{1,0:T(8,128)} %panel.3) | copy-start | bytes 491524
  77.5 1.5 copy-start.1
  139.5 9.4 %all-to-all-start.2 = ((f32[8,64,128]{2,1,0:T(8,128)}), f32[8,64,128]{2,1,0:T(8,128)S(1)}, u32[]{:S(2)}, u32[]{:S(2)}) async-start(f32[8,64,128]{2,1,0:T(8,128)} %broadcast_in_dim.7), calls=%async_computation.2 | async-start | bytes 524288 | tf_op jit(solution)/shard_map/all_to_all | solution.py:170
  150.6 36.3 %all-to-all-start.3 = ((f32[8,16,40,128]{3,2,1,0:T(8,128)}), f32[8,16,40,128]{3,2,1,0:T(8,128)}, u32[]{:S(2)}, u32[]{:S(2)}) async-start(f32[8,16,40,128]{3,2,1,0:T(8,128)} %broadcast_in_dim.8), calls=%async_computation.3 | async-start | bytes 5242880 | tf_op jit(solution)/shard_map/all_to_all | solution.py:170
  186.9 1.7 copy-start.2

commit v3 on v2

--- a/solution.py
+++ b/solution.py
@@ -15,7 +15,10 @@
 FAR, NEAR, XS, YS, CORES = 16, 2, 4, 4, 2
 GROUPS = NEAR * XS
 COLS = YS * CORES
+CHUNKS = 4
+NARROW = FAR // CHUNKS
 VMEM = pl.BlockSpec(memory_space=pltpu.VMEM)
+HBM = pl.BlockSpec(memory_space=pltpu.HBM)
 PARAMS = pltpu.CompilerParams(vmem_limit_bytes=48 * 1024 * 1024)
 
 
@@ -49,26 +52,38 @@
     return jnp.concatenate([value[:, i * LANES : (i + 1) * LANES] for i in range(HALVES)], axis=0)
 
 
-def assemble(pieces, far, base, rows, target):
-    for half in range(HALVES):
-        lo = base + half * FINE
-        target[rows, half * LANES : (half + 1) * LANES] = jnp.concatenate(
-            [pieces[g, far, lo : lo + FINE, :] for g in range(GROUPS)], axis=0
-        )
-
-
-def first_kernel(stored, gathered, panel, columns, payload):
-    far_rows = GROUPS * FINE
-
-    @pl.loop(0, FAR)
-    def _(far):
-        assemble(gathered, far, 0, pl.ds(pl.multiple_of(far * far_rows, 8), far_rows), columns)
-
-    wide = far_rows * 4
+def fetch(pieces, landing, arrived, chunk):
+    return pltpu.make_async_copy(
+        pieces.at[:, pl.ds(chunk * NARROW, NARROW)], landing.at[chunk], arrived.at[chunk]
+    )
+
+
+def assemble(landing, chunk):
+    return jnp.concatenate(
+        [
+            jnp.concatenate(
+                [landing[chunk, g, far, half * FINE : (half + 1) * FINE, :] for far in range(NARROW) for g in range(GROUPS)],
+                axis=0,
+            )
+            for half in range(HALVES)
+        ],
+        axis=1,
+    )
+
+
+def first_kernel(stored, gathered, panel, columns, payload, landing, held, arrived, left):
+    wide = NARROW * GROUPS * FINE
+    for i in range(CHUNKS):
+        fetch(gathered, landing, arrived, i).start()
     image = jnp.zeros((panel.shape[0], BAND), jnp.float32)
     gram = jnp.zeros((BAND, BAND), jnp.float32)
-    for i in range(stored.shape[1] // wide):
-        part = columns[i * wide : (i + 1) * wide, :]
+    outgoing = []
+    for i in range(CHUNKS):
+        fetch(gathered, landing, arrived, i).wait()
+        part = assemble(landing, i)
+        held[i] = part
+        outgoing.append(pltpu.make_async_copy(held.at[i], columns.at[i], left.at[i]))
+        outgoing[-1].start()
         image += three_pass(split(stored[:, i * wide : (i + 1) * wide]), split(part), ((1,), (0,)))
         gram += precise(part, part, ((0,), (0,)))
     cross = precise(panel[...], image, ((0,), (0,)))
@@ -77,6 +92,8 @@
         payload[c, :PIECE, :] = stack_halves(image[c * FINE : (c + 1) * FINE, :])
         payload[c, PIECE : PIECE + SLICE, :] = stack_halves(gram[c * eighth : (c + 1) * eighth, :])
         payload[c, PIECE + SLICE :, :] = stack_halves(cross[c * eighth : (c + 1) * eighth, :])
+    for copy in outgoing:
+        copy.wait()
 
 
 def eliminate(block):
@@ -142,82 +159,110 @@
     return precise(precise(value, unit, ((1,), (1,))), scaled, ((1,), (0,)))
 
 
-def second_kernel(panel, small, unit, scaled, left, work):
+def second_kernel(panel, small, left, right, work, scaled):
     invert(unstack(small, PIECE, BAND // COLS), work, scaled)
-    unit[...] = work[:, BAND:]
-    left[...] = 2.0 * by_inverse(panel[...], unit[...], scaled[...])
-
-
-def third_kernel(stored, left, unit, scaled, small, columns, pieces, out, image):
-    far_rows = GROUPS * FINE
-
-    @pl.loop(0, FAR)
-    def _(far):
-        assemble(pieces, far, 0, pl.ds(pl.multiple_of(far * far_rows, 8), far_rows), image)
-
+    unit, over = work[:, BAND:], scaled[...]
+    first = 2.0 * by_inverse(panel[...], unit, over)
+    left[...] = first
+    own = unstack(small, 0, FINE)
     cross = unstack(small, PIECE + SLICE, BAND // COLS)
-    own = unstack(small, 0, FINE) - precise(left[...], cross, ((1,), (0,)))
-    a, b = split(left[...]), split(2.0 * by_inverse(own, unit[...], scaled[...]))
-    wide = far_rows * 4
-    for i in range(stored.shape[1] // wide):
-        at = slice(i * wide, (i + 1) * wide)
-        out[:, at] = stored[:, at] - (
-            three_pass(a, split(image[at, :]), ((1,), (1,))) + three_pass(b, split(columns[at, :]), ((1,), (1,)))
-        )
-
-
-def spread(value, axes, count):
-    return lax.all_to_all(jnp.broadcast_to(value[None], (count, *value.shape)), axes, 0, 0)
+    right[...] = 2.0 * by_inverse(own - precise(first, cross, ((1,), (0,))), unit, over)
+
+
+def third_kernel(stored, left, right, columns, pieces, out, landing, held, result, arrived, brought, gone):
+    wide = NARROW * GROUPS * FINE
+    bring = [pltpu.make_async_copy(columns.at[i], held.at[i], brought.at[i]) for i in range(CHUNKS)]
+    for i in range(CHUNKS):
+        bring[i].start()
+        fetch(pieces, landing, arrived, i).start()
+    a, b = split(left[...]), split(right[...])
+    outgoing = []
+    for i in range(CHUNKS):
+        at = pl.ds(i * wide, wide)
+        bring[i].wait()
+        total = three_pass(b, split(held[i]), ((1,), (1,)))
+        fetch(pieces, landing, arrived, i).wait()
+        total += three_pass(a, split(assemble(landing, i)), ((1,), (1,)))
+        result[i] = stored[:, at] - total
+        outgoing.append(pltpu.make_async_copy(result.at[i], out.at[:, at], gone.at[i]))
+        outgoing[-1].start()
+    for copy in outgoing:
+        copy.wait()
+
+
+def copies(value, count):
+    return jnp.broadcast_to(value[None], (count, *value.shape))
+
+
+def spread_kernel(far, out, gone):
+    copies = [pltpu.make_async_copy(far.at[:, pl.ds(0, PIECE)], out.at[g], gone.at[g]) for g in range(GROUPS)]
+    for copy in copies:
+        copy.start()
+    for copy in copies:
+        copy.wait()
 
 
 def on_device(stored, panel):
     f32 = jnp.float32
     rows, width = stored.shape
+    wide = width // CHUNKS
     col = ("y", "core")
     group = ("near", "x")
     c = lax.axis_index(col)
-    pieces_shape = (GROUPS, FAR, PIECE, LANES)
+    semaphores = pltpu.SemaphoreType.DMA((CHUNKS,))
+    landing = pltpu.VMEM((CHUNKS, GROUPS, NARROW, PIECE, LANES), f32)
+    held = pltpu.VMEM((CHUNKS, wide, BAND), f32)
     own = stack_halves(lax.dynamic_slice_in_dim(panel, c * FINE, FINE, 0))
-    gathered = spread(lax.all_gather(own, "far", axis=0), group, GROUPS)
+    gathered = lax.all_to_all(copies(lax.all_gather(own, "far", axis=0), GROUPS), group, 0, 0)
     columns, payload = pl.pallas_call(
         first_kernel,
         out_shape=(
-            jax.ShapeDtypeStruct((width, BAND), f32),
+            pltpu.HBM((CHUNKS, wide, BAND), f32),
             jax.ShapeDtypeStruct((COLS, PIECE + 2 * SLICE, LANES), f32),
         ),
-        in_specs=[VMEM] * 3,
-        out_specs=(VMEM, VMEM),
+        in_specs=[VMEM, HBM, VMEM],
+        out_specs=(HBM, VMEM),
+        scratch_shapes=[landing, held, semaphores, semaphores],
         compiler_params=PARAMS,
         name="image_and_gram",
     )(stored, gathered, panel)
     summed = jnp.sum(lax.all_to_all(payload, col, 0, 0), axis=0)
     far = lax.all_gather(jnp.concatenate([summed[:PIECE], summed[PIECE + SLICE :]], axis=0), "far", axis=0)
-    parts = spread(jnp.sum(far[:, PIECE:, :], axis=0), group, GROUPS)
-    image_far, parts = lax.optimization_barrier((far[:, :PIECE, :], parts))
-    image = spread(image_far, group, GROUPS)
+    parts = lax.all_to_all(copies(jnp.sum(far[:, PIECE:, :], axis=0), GROUPS), group, 0, 0)
+    image = pl.pallas_call(
+        spread_kernel,
+        out_shape=pltpu.HBM((GROUPS, FAR, PIECE, LANES), f32),
+        in_specs=[VMEM],
+        out_specs=HBM,
+        scratch_shapes=[pltpu.SemaphoreType.DMA((GROUPS,))],
+        compiler_params=PARAMS,
+        cost_estimate=pl.CostEstimate(flops=10**10, bytes_accessed=3 * 10**6, transcendentals=0),
+        name="image_copies",
+    )(far)
+    image, parts = lax.optimization_barrier((image, parts))
+    image = lax.all_to_all(image, group, 0, 0)
     small = lax.all_gather(
         jnp.concatenate([summed[: PIECE + SLICE], jnp.sum(parts, axis=0)], axis=0), col, axis=0
     )
-    square = jax.ShapeDtypeStruct((BAND, BAND), f32)
-    unit, scaled, left = pl.pallas_call(
+    left, right = pl.pallas_call(
         second_kernel,
-        out_shape=(square, square, jax.ShapeDtypeStruct((rows, BAND), f32)),
+        out_shape=(jax.ShapeDtypeStruct((rows, BAND), f32),) * 2,
         in_specs=[VMEM] * 2,
-        out_specs=(VMEM,) * 3,
-        scratch_shapes=[pltpu.VMEM((BAND, 2 * BAND), f32)],
+        out_specs=(VMEM,) * 2,
+        scratch_shapes=[pltpu.VMEM((BAND, 2 * BAND), f32), pltpu.VMEM((BAND, BAND), f32)],
         compiler_params=PARAMS,
         cost_estimate=pl.CostEstimate(flops=10**10, bytes_accessed=2 * 10**6, transcendentals=0),
-        name="factorization",
+        name="row_factors",
     )(panel, small)
     return pl.pallas_call(
         third_kernel,
         out_shape=jax.ShapeDtypeStruct((rows, width), f32),
-        in_specs=[VMEM] * 7,
-        out_specs=VMEM,
-        scratch_shapes=[pltpu.VMEM((width, BAND), f32)],
+        in_specs=[VMEM] * 3 + [HBM] * 2,
+        out_specs=HBM,
+        scratch_shapes=[landing, held, pltpu.VMEM((CHUNKS, rows, wide), f32)] + [semaphores] * 3,
         compiler_params=PARAMS,
         name="update",
-    )(stored, left, unit, scaled, small, columns, image)
+    )(stored, left, right, columns, image)
 
 
 def solution(mesh):

time: 196 us -> 194 us (0.990)
  local copies, waits for them, and re-layouts: 6.66 us -> 3.46 us
  Pallas kernels: 23 us -> 25.7 us
    pallas_call x2 -> x3, Pallas kernels: 16.3 us -> 18.8 us  [the longest x1 11.5 us: on_device(): pl.pallas_call(second_kernel, out_shape=(jax.ShapeDtypeStruct((rows, BAND...]
  transfers between devices with their start and end apart: 2 -> 2, of which waited for: 1 -> 1; matrix products, arithmetic and copies ran while one was open for 0% -> 0% of each run, Pallas kernels for 5% -> 7%
where the time goes in v3:
time: 194 us; the launch traced here: 193 us
  blocking collectives  152 us (78%)
  Pallas kernels  25.7 us (13%)
  starting transfers between devices  7.81 us (4%)
  waiting for transfers between devices  4.41 us (2%)
  local copies, waits for them, and re-layouts  3.46 us (2%)
    all_gather x1, blocking collectives, on_device(): lax.all_gather(own, 'far', axis=0)  43 us
    all_gather x1, blocking collectives, on_device(): lax.all_gather(jnp.concatenate([summed[:PIECE], summed[PIECE + SLICE:]],...  34.1 us
    all_to_all x1, blocking collectives, on_device(): lax.all_to_all(copies(lax.all_gather(own, 'far', axis=0), GROUPS), group,...  27.5 us
    all_to_all x1, blocking collectives, on_device(): summed = jnp.sum(lax.all_to_all(payload, col, 0, 0), axis=0)  25.5 us
    all_gather x1, blocking collectives, on_device(): lax.all_gather(jnp.concatenate([summed[:PIECE + SLICE], jnp.sum(parts, ax...  21.5 us
    pallas_call x1, Pallas kernels, on_device(): pl.pallas_call(second_kernel, out_shape=(jax.ShapeDtypeStruct((rows, BAND...  11.5 us
    pallas_call x1, Pallas kernels, on_device(): pl.pallas_call(third_kernel, out_shape=jax.ShapeDtypeStruct((rows, width)...  6.91 us
    pallas_call x1, Pallas kernels, on_device(): pl.pallas_call(first_kernel, out_shape=(pltpu.HBM((CHUNKS, wide, BAND), f...  5.63 us
  transfers between devices with their start and end apart: 2, of which 1 were waited for; matrix products, arithmetic and copies ran while one was open for 0% of the time, Pallas kernels for 7%

profile of v3, /device:TPU:1, one launch (start us, length us, event | category | flops | bytes accessed | tf_op | source)
XLA Modules:
  0.0 193.4 jit_solution(14102425415131649180)
XLA Ops:
  0.0 0.8 constant_dynamic-slice_fusion
  0.8 43.0 %all-gather = f32[640,128]{1,0:T(8,128)S(1)} all-gather(f32[40,128]{1,0:T(8,128)S(1)} %pad_maximum_fusion.2), channel_id=2, replica_groups=mesh['far'=16,'near'=2,'x'=4,'y'=4,'core'=2] {'far'}, dimensions={0}, use_global_device_ids=true | all-gather | bytes 348160 | tf_op jit(solution)/shard_map/all_gather | solution.py:216
  43.8 0.2 broadcast_in_dim.4
  44.0 0.0 copy-start
  44.0 0.0 copy-start.2
  44.0 27.5 %all_to_all.20.gathered = f32[8,16,40,128]{3,2,1,0:T(8,128)S(1)} all-to-all(f32[8,16,40,128]{3,2,1,0:T(8,128)S(1)} %broadcast_in_dim.4), channel_id=1, replica_groups=mesh['far'=16,'near'=2,'x'=4,'y'=4,'core'=2] {'near','x'}, dimensions={0} | all-to-all | bytes 5242880 | tf_op jit(solution)/shard_map/all_to_all | solution.py:216
  71.5 0.0 copy-done
  71.5 0.0 copy-done.2
  71.5 5.6 %image_and_gram.1 = (f32[4,640,256]{2,1,0:T(8,128)}, f32[8,168,128]{2,1,0:T(8,128)S(1)}) custom-call(f32[160,2560]{1,0:T(8,128)S(1)} %copy-done, f32[8,16,40,128]{3,2,1,0:T(8,128)S(1)} %all_to_all.20.gathered, f32[160,256]{1,0:T(8,128)S(1)} %copy-done.2), custom_call_target="tpu_custom_call" | custom-call | tf_op jit(solution)/shard_map/image_and_gram/pallas_call | solution.py:217
  77.2 25.5 %all_to_all.21 = f32[8,168,128]{2,1,0:T(8,128)S(1)} all-to-all(f32[8,168,128]{2,1,0:T(8,128)S(1)} %get-tuple-element.11), channel_id=1, replica_groups=mesh['far'=16,'near'=2,'x'=4,'y'=4,'core'=2] {'y','core'}, dimensions={0} | all-to-all | bytes 1376256 | tf_op jit(solution)/shard_map/all_to_all | solution.py:229
  102.8 34.1 %all-gather.1 = f32[1664,128]{1,0:T(8,128)S(1)} all-gather(f32[104,128]{1,0:T(8,128)S(1)} %pad_maximum_fusion.1), channel_id=3, replica_groups=mesh['far'=16,'near'=2,'x'=4,'y'=4,'core'=2] {'far'}, dimensions={0}, use_global_device_ids=true | all-gather | bytes 905216 | tf_op jit(solution)/shard_map/all_gather | solution.py:230
  137.0 0.7 broadcast_in_dim.5
  137.7 3.4 %all-to-all-start.2 = ((f32[8,64,128]{2,1,0:T(8,128)}), f32[8,64,128]{2,1,0:T(8,128)S(1)}, u32[]{:S(2)}, u32[]{:S(2)}) async-start(f32[8,64,128]{2,1,0:T(8,128)} %broadcast_in_dim.5), calls=%async_computation.2 | async-start | bytes 524288 | tf_op jit(solution)/shard_map/all_to_all | solution.py:231
  141.1 1.6 image_copies.1
  142.7 4.4 %all-to-all-done.2 = f32[8,64,128]{2,1,0:T(8,128)S(1)} async-done(((f32[8,64,128]{2,1,0:T(8,128)}), f32[8,64,128]{2,1,0:T(8,128)S(1)}, u32[]{:S(2)}, u32[]{:S(2)}) %all-to-all-start.2) | async-done | bytes 262176 | tf_op jit(solution)/shard_map/all_to_all | solution.py:231
  147.1 4.4 %all-to-all-start.3 = ((f32[8,16,40,128]{3,2,1,0:T(8,128)}), f32[8,16,40,128]{3,2,1,0:T(8,128)}, u32[]{:S(2)}, u32[]{:S(2)}) async-start(f32[8,16,40,128]{3,2,1,0:T(8,128)} %image_copies.1), calls=%async_computation.3 | async-start | bytes 5242880 | tf_op jit(solution)/shard_map/all_to_all | solution.py:243
  151.6 21.5 %all-gather.2 = f32[1344,128]{1,0:T(8,128)S(1)} all-gather(f32[168,128]{1,0:T(8,128)S(1)} %pad_maximum_fusion), channel_id=4, replica_groups=mesh['far'=16,'near'=2,'x'=4,'y'=4,'core'=2] {'y','core'}, dimensions={0}, use_global_device_ids=true | all-gather | bytes 774144 | tf_op jit(solution)/shard_map/all_gather | solution.py:244
  173.0 11.5 %row_factors.1 = (f32[160,256]{1,0:T(8,128)S(1)}, f32[160,256]{1,0:T(8,128)S(1)}) custom-call(f32[160,256]{1,0:T(8,128)S(1)} %copy-done.2, f32[8,168,128]{2,1,0:T(8,128)S(1)} %bitcast.5), custom_call_target="tpu_custom_call" | custom-call | flops 10000000000 | bytes 2000000 | tf_op jit(solution)/shard_map/row_factors/pallas_call | solution.py:247
  184.6 0.0 all-to-all-done.3.pieces
  184.6 0.0 copy-start.1
  184.6 1.7 copy-done.1
  186.3 6.9 %update.1 = f32[160,2560]{1,0:T(8,128)} custom-call(f32[160,2560]{1,0:T(8,128)S(1)} %copy-done, f32[160,256]{1,0:T(8,128)S(1)} %get-tuple-element.13.left, f32[160,256]{1,0:T(8,128)S(1)} %get-tuple-element.14.right, f32[4,640,256]{2,1,0:T(8,128)S(1)} %copy-done.1, f32[8,16,40,128]{3,2,1,0:T(8,128)} %all-to-all-done.3.pieces), custom_call_target="tpu_custom_call" | custom-call | tf_op jit(solution)/shard_map/update/pallas_call | solution.py:257
  (9 shorter events, 0.1 us)
Async XLA Ops:
  44.0 27.5 %copy-start = (f32[160,2560]{1,0:T(8,128)S(1)}, f32[160,2560]{1,0:T(8,128)}, u32[]{:S(2)}) copy-start(f32[160,2560]{1,0:T(8,128)} %stored.3) | copy-start | bytes 4915204
  44.0 27.5 %copy-start.2 = (f32[160,256]{1,0:T(8,128)S(1)}, f32[160,256]{1,0:T(8,128)}, u32[]{:S(2)}) copy-start(f32[160,256]{1,0:T(8,128)} %panel.3) | copy-start | bytes 491524
  137.7 9.4 %all-to-all-start.2 = ((f32[8,64,128]{2,1,0:T(8,128)}), f32[8,64,128]{2,1,0:T(8,128)S(1)}, u32[]{:S(2)}, u32[]{:S(2)}) async-start(f32[8,64,128]{2,1,0:T(8,128)} %broadcast_in_dim.5), calls=%async_computation.2 | async-start | bytes 524288 | tf_op jit(solution)/shard_map/all_to_all | solution.py:231
  147.1 37.5 %all-to-all-start.3 = ((f32[8,16,40,128]{3,2,1,0:T(8,128)}), f32[8,16,40,128]{3,2,1,0:T(8,128)}, u32[]{:S(2)}, u32[]{:S(2)}) async-start(f32[8,16,40,128]{3,2,1,0:T(8,128)} %image_copies.1), calls=%async_computation.3 | async-start | bytes 5242880 | tf_op jit(solution)/shard_map/all_to_all | solution.py:243
  184.6 1.7 copy-start.1

commit v4 on v3

--- a/solution.py
+++ b/solution.py
@@ -39,31 +39,25 @@
     return high, (value - high.astype(jnp.float32)).astype(jnp.bfloat16)
 
 
-def three_pass(left, right, dims):
+def one_pass(left, right):
+    return lax.dot_general(left, right, (((1,), (0,)), ((), ())), preferred_element_type=jnp.float32)
+
+
+def three_pass(left, right):
     (lh, ll), (rh, rl) = left, right
-
-    def one(a, b):
-        return lax.dot_general(a, b, (dims, ((), ())), preferred_element_type=jnp.float32)
-
-    return (one(lh, rl) + one(ll, rh)) + one(lh, rh)
+    return (one_pass(lh, rl) + one_pass(ll, rh)) + one_pass(lh, rh)
 
 
 def stack_halves(value):
     return jnp.concatenate([value[:, i * LANES : (i + 1) * LANES] for i in range(HALVES)], axis=0)
 
 
-def fetch(pieces, landing, arrived, chunk):
-    return pltpu.make_async_copy(
-        pieces.at[:, pl.ds(chunk * NARROW, NARROW)], landing.at[chunk], arrived.at[chunk]
-    )
-
-
-def assemble(landing, chunk):
+def assemble(pieces, chunk):
+    fars = range(chunk * NARROW, (chunk + 1) * NARROW)
     return jnp.concatenate(
         [
             jnp.concatenate(
-                [landing[chunk, g, far, half * FINE : (half + 1) * FINE, :] for far in range(NARROW) for g in range(GROUPS)],
-                axis=0,
+                [pieces[g, far, half * FINE : (half + 1) * FINE, :] for far in fars for g in range(GROUPS)], axis=0
             )
             for half in range(HALVES)
         ],
@@ -71,21 +65,25 @@
     )
 
 
-def first_kernel(stored, gathered, panel, columns, payload, landing, held, arrived, left):
+def first_kernel(stored, gathered, panel, columns, payload, held, gone):
+    f32 = jnp.float32
     wide = NARROW * GROUPS * FINE
-    for i in range(CHUNKS):
-        fetch(gathered, landing, arrived, i).start()
-    image = jnp.zeros((panel.shape[0], BAND), jnp.float32)
-    gram = jnp.zeros((BAND, BAND), jnp.float32)
+    image = jnp.zeros((panel.shape[0], BAND), f32)
+    even, odd = jnp.zeros((BAND, BAND), f32), jnp.zeros((BAND, BAND), f32)
     outgoing = []
     for i in range(CHUNKS):
-        fetch(gathered, landing, arrived, i).wait()
-        part = assemble(landing, i)
-        held[i] = part
-        outgoing.append(pltpu.make_async_copy(held.at[i], columns.at[i], left.at[i]))
+        part = assemble(gathered, i)
+        turned = part.T
+        held[i] = turned
+        outgoing.append(pltpu.make_async_copy(held.at[i], columns.at[i], gone.at[i]))
         outgoing[-1].start()
-        image += three_pass(split(stored[:, i * wide : (i + 1) * wide]), split(part), ((1,), (0,)))
-        gram += precise(part, part, ((0,), (0,)))
+        high, middle = split(part)
+        low = (part - high.astype(f32) - middle.astype(f32)).astype(jnp.bfloat16)
+        turned_high, turned_middle = split(turned)
+        image += three_pass(split(stored[:, i * wide : (i + 1) * wide]), (high, middle))
+        even += one_pass(turned_high, high) + one_pass(turned_middle, middle)
+        odd += one_pass(turned_high, middle) + one_pass(turned_high, low)
+    gram = even + (odd + odd.T)
     cross = precise(panel[...], image, ((0,), (0,)))
     eighth = BAND // COLS
     for c in range(COLS):
@@ -169,25 +167,29 @@
     right[...] = 2.0 * by_inverse(own - precise(first, cross, ((1,), (0,))), unit, over)
 
 
-def third_kernel(stored, left, right, columns, pieces, out, landing, held, result, arrived, brought, gone):
+def third_kernel(stored, left, right, columns, pieces, out, tile, held, result, brought, fetched, gone):
     wide = NARROW * GROUPS * FINE
+    parts = [pl.ds(i * wide, wide) for i in range(CHUNKS)]
     bring = [pltpu.make_async_copy(columns.at[i], held.at[i], brought.at[i]) for i in range(CHUNKS)]
+    fetch = [pltpu.make_async_copy(stored.at[:, parts[i]], tile.at[i], fetched.at[i]) for i in range(CHUNKS)]
+    for copy in bring + fetch:
+        copy.start()
+    a, b = split(left[...]), split(right[...])
     for i in range(CHUNKS):
-        bring[i].start()
-        fetch(pieces, landing, arrived, i).start()
-    a, b = split(left[...]), split(right[...])
+        result[i] = three_pass(a, split(assemble(pieces, i).T))
+    for copy in bring + fetch:
+        copy.wait()
     outgoing = []
     for i in range(CHUNKS):
-        at = pl.ds(i * wide, wide)
-        bring[i].wait()
-        total = three_pass(b, split(held[i]), ((1,), (1,)))
-        fetch(pieces, landing, arrived, i).wait()
-        total += three_pass(a, split(assemble(landing, i)), ((1,), (1,)))
-        result[i] = stored[:, at] - total
-        outgoing.append(pltpu.make_async_copy(result.at[i], out.at[:, at], gone.at[i]))
+        result[i] = tile[i] - (result[i] + three_pass(b, split(held[i])))
+        outgoing.append(pltpu.make_async_copy(result.at[i], out.at[:, parts[i]], gone.at[i]))
         outgoing[-1].start()
     for copy in outgoing:
         copy.wait()
+
+
+def in_hbm(value):
+    return pltpu.with_memory_space_constraint(value, pltpu.HBM)
 
 
 def copies(value, count):
@@ -210,19 +212,19 @@
     group = ("near", "x")
     c = lax.axis_index(col)
     semaphores = pltpu.SemaphoreType.DMA((CHUNKS,))
-    landing = pltpu.VMEM((CHUNKS, GROUPS, NARROW, PIECE, LANES), f32)
-    held = pltpu.VMEM((CHUNKS, wide, BAND), f32)
+    held = pltpu.VMEM((CHUNKS, BAND, wide), f32)
+    tile = pltpu.VMEM((CHUNKS, rows, wide), f32)
     own = stack_halves(lax.dynamic_slice_in_dim(panel, c * FINE, FINE, 0))
     gathered = lax.all_to_all(copies(lax.all_gather(own, "far", axis=0), GROUPS), group, 0, 0)
     columns, payload = pl.pallas_call(
         first_kernel,
         out_shape=(
-            pltpu.HBM((CHUNKS, wide, BAND), f32),
+            pltpu.HBM((CHUNKS, BAND, wide), f32),
             jax.ShapeDtypeStruct((COLS, PIECE + 2 * SLICE, LANES), f32),
         ),
-        in_specs=[VMEM, HBM, VMEM],
+        in_specs=[VMEM] * 3,
         out_specs=(HBM, VMEM),
-        scratch_shapes=[landing, held, semaphores, semaphores],
+        scratch_shapes=[held, semaphores],
         compiler_params=PARAMS,
         name="image_and_gram",
     )(stored, gathered, panel)
@@ -257,12 +259,12 @@
     return pl.pallas_call(
         third_kernel,
         out_shape=jax.ShapeDtypeStruct((rows, width), f32),
-        in_specs=[VMEM] * 3 + [HBM] * 2,
+        in_specs=[HBM, VMEM, VMEM, HBM, VMEM],
         out_specs=HBM,
-        scratch_shapes=[landing, held, pltpu.VMEM((CHUNKS, rows, wide), f32)] + [semaphores] * 3,
+        scratch_shapes=[tile, held, tile] + [semaphores] * 3,
         compiler_params=PARAMS,
         name="update",
-    )(stored, left, right, columns, image)
+    )(in_hbm(stored), left, right, in_hbm(columns), image)
 
 
 def solution(mesh):

time: 194 us -> 186 us (0.959)
  Pallas kernels: 25.7 us -> 20.2 us
    pallas_call x1, Pallas kernels: 6.91 us -> 4.04 us  [on_device(): pl.pallas_call(third_kernel, out_shape=jax.ShapeDtypeStruct((rows, width)...]
    pallas_call x1, Pallas kernels: 5.63 us -> 3.03 us  [on_device(): pl.pallas_call(first_kernel, out_shape=(pltpu.HBM((CHUNKS, BAND, wide), f...]
where the time goes in v4:
time: 186 us; the launch traced here: 185 us
  blocking collectives  152 us (82%)
  Pallas kernels  20.2 us (11%)
  starting transfers between devices  7.04 us (4%)
  waiting for transfers between devices  4.4 us (2%)
    all_gather x1, blocking collectives, on_device(): lax.all_gather(own, 'far', axis=0)  43 us
    all_gather x1, blocking collectives, on_device(): lax.all_gather(jnp.concatenate([summed[:PIECE], summed[PIECE + SLICE:]],...  34.1 us
    all_to_all x1, blocking collectives, on_device(): lax.all_to_all(copies(lax.all_gather(own, 'far', axis=0), GROUPS), group,...  27.5 us
    all_to_all x1, blocking collectives, on_device(): summed = jnp.sum(lax.all_to_all(payload, col, 0, 0), axis=0)  25.5 us
    all_gather x1, blocking collectives, on_device(): lax.all_gather(jnp.concatenate([summed[:PIECE + SLICE], jnp.sum(parts, ax...  21.5 us
    pallas_call x1, Pallas kernels, on_device(): pl.pallas_call(second_kernel, out_shape=(jax.ShapeDtypeStruct((rows, BAND...  11.5 us
    all_to_all x1, waiting for transfers between devices, on_device(): lax.all_to_all(copies(jnp.sum(far[:, PIECE:, :], axis=0), GROUPS), group,...  4.4 us
    pallas_call x1, Pallas kernels, on_device(): pl.pallas_call(third_kernel, out_shape=jax.ShapeDtypeStruct((rows, width)...  4.04 us
  transfers between devices with their start and end apart: 2, of which 1 were waited for; matrix products, arithmetic and copies ran while one was open for 0% of the time, Pallas kernels for 7%

profile of v4, /device:TPU:1, one launch (start us, length us, event | category | flops | bytes accessed | tf_op | source)
XLA Modules:
  0.0 185.4 jit_solution(17527248074554348231)
XLA Ops:
  0.0 0.8 constant_dynamic-slice_fusion
  0.8 43.0 %all-gather = f32[640,128]{1,0:T(8,128)S(1)} all-gather(f32[40,128]{1,0:T(8,128)S(1)} %pad_maximum_fusion.2), channel_id=2, replica_groups=mesh['far'=16,'near'=2,'x'=4,'y'=4,'core'=2] {'far'}, dimensions={0}, use_global_device_ids=true | all-gather | bytes 348160 | tf_op jit(solution)/shard_map/all_gather | solution.py:218
  43.8 0.2 broadcast_in_dim.4
  44.0 0.0 copy-start
  44.0 0.0 copy-start.1
  44.0 27.5 %all_to_all.20.gathered = f32[8,16,40,128]{3,2,1,0:T(8,128)S(1)} all-to-all(f32[8,16,40,128]{3,2,1,0:T(8,128)S(1)} %broadcast_in_dim.4), channel_id=1, replica_groups=mesh['far'=16,'near'=2,'x'=4,'y'=4,'core'=2] {'near','x'}, dimensions={0} | all-to-all | bytes 5242880 | tf_op jit(solution)/shard_map/all_to_all | solution.py:218
  71.5 0.0 copy-done
  71.5 0.0 copy-done.1
  71.5 3.0 %image_and_gram.1 = (f32[4,256,640]{2,1,0:T(8,128)}, f32[8,168,128]{2,1,0:T(8,128)S(1)}) custom-call(f32[160,2560]{1,0:T(8,128)S(1)} %copy-done, f32[8,16,40,128]{3,2,1,0:T(8,128)S(1)} %all_to_all.20.gathered, f32[160,256]{1,0:T(8,128)S(1)} %copy-done.1), custom_call_target="tpu_custom_call" | custom-call | tf_op jit(solution)/shard_map/image_and_gram/pallas_call | solution.py:219
  74.6 25.5 %all_to_all.21 = f32[8,168,128]{2,1,0:T(8,128)S(1)} all-to-all(f32[8,168,128]{2,1,0:T(8,128)S(1)} %get-tuple-element.11), channel_id=1, replica_groups=mesh['far'=16,'near'=2,'x'=4,'y'=4,'core'=2] {'y','core'}, dimensions={0} | all-to-all | bytes 1376256 | tf_op jit(solution)/shard_map/all_to_all | solution.py:231
  100.2 34.1 %all-gather.1 = f32[1664,128]{1,0:T(8,128)S(1)} all-gather(f32[104,128]{1,0:T(8,128)S(1)} %pad_maximum_fusion.1), channel_id=3, replica_groups=mesh['far'=16,'near'=2,'x'=4,'y'=4,'core'=2] {'far'}, dimensions={0}, use_global_device_ids=true | all-gather | bytes 905216 | tf_op jit(solution)/shard_map/all_gather | solution.py:232
  134.3 0.7 broadcast_in_dim.5
  135.1 3.4 %all-to-all-start.2 = ((f32[8,64,128]{2,1,0:T(8,128)}), f32[8,64,128]{2,1,0:T(8,128)S(1)}, u32[]{:S(2)}, u32[]{:S(2)}) async-start(f32[8,64,128]{2,1,0:T(8,128)} %broadcast_in_dim.5), calls=%async_computation.2 | async-start | bytes 524288 | tf_op jit(solution)/shard_map/all_to_all | solution.py:233
  138.5 1.6 image_copies.1
  140.1 4.4 %all-to-all-done.2 = f32[8,64,128]{2,1,0:T(8,128)S(1)} async-done(((f32[8,64,128]{2,1,0:T(8,128)}), f32[8,64,128]{2,1,0:T(8,128)S(1)}, u32[]{:S(2)}, u32[]{:S(2)}) %all-to-all-start.2) | async-done | bytes 262176 | tf_op jit(solution)/shard_map/all_to_all | solution.py:233
  144.5 3.6 %all-to-all-start.3 = ((f32[8,16,40,128]{3,2,1,0:T(8,128)}), f32[8,16,40,128]{3,2,1,0:T(8,128)S(1)}, u32[]{:S(2)}, u32[]{:S(2)}) async-start(f32[8,16,40,128]{3,2,1,0:T(8,128)} %image_copies.1), calls=%async_computation.3 | async-start | bytes 5242880 | tf_op jit(solution)/shard_map/all_to_all | solution.py:245
  148.2 21.5 %all-gather.2 = f32[1344,128]{1,0:T(8,128)S(1)} all-gather(f32[168,128]{1,0:T(8,128)S(1)} %pad_maximum_fusion), channel_id=4, replica_groups=mesh['far'=16,'near'=2,'x'=4,'y'=4,'core'=2] {'y','core'}, dimensions={0}, use_global_device_ids=true | all-gather | bytes 774144 | tf_op jit(solution)/shard_map/all_gather | solution.py:246
  169.7 11.5 %row_factors.1 = (f32[160,256]{1,0:T(8,128)S(1)}, f32[160,256]{1,0:T(8,128)S(1)}) custom-call(f32[160,256]{1,0:T(8,128)S(1)} %copy-done.1, f32[8,168,128]{2,1,0:T(8,128)S(1)} %bitcast.5), custom_call_target="tpu_custom_call" | custom-call | flops 10000000000 | bytes 2000000 | tf_op jit(solution)/shard_map/row_factors/pallas_call | solution.py:249
  181.2 0.0 all-to-all-done.3.pieces
  181.2 4.0 %update.1 = f32[160,2560]{1,0:T(8,128)} custom-call(f32[160,2560]{1,0:T(8,128)} %stored.3, f32[160,256]{1,0:T(8,128)S(1)} %get-tuple-element.13.left, f32[160,256]{1,0:T(8,128)S(1)} %get-tuple-element.14.right, f32[4,256,640]{2,1,0:T(8,128)} %get-tuple-element.15.columns, f32[8,16,40,128]{3,2,1,0:T(8,128)S(1)} %all-to-all-done.3.pieces), custom_call_target="tpu_custom_call" | custom-call | tf_op jit(solution)/shard_map/update/pallas_call | solution.py:259
  (9 shorter events, 0.1 us)
Async XLA Ops:
  44.0 27.5 %copy-start = (f32[160,2560]{1,0:T(8,128)S(1)}, f32[160,2560]{1,0:T(8,128)}, u32[]{:S(2)}) copy-start(f32[160,2560]{1,0:T(8,128)} %stored.3) | copy-start | bytes 4915204
  44.0 27.5 %copy-start.1 = (f32[160,256]{1,0:T(8,128)S(1)}, f32[160,256]{1,0:T(8,128)}, u32[]{:S(2)}) copy-start(f32[160,256]{1,0:T(8,128)} %panel.3) | copy-start | bytes 491524
  135.1 9.4 %all-to-all-start.2 = ((f32[8,64,128]{2,1,0:T(8,128)}), f32[8,64,128]{2,1,0:T(8,128)S(1)}, u32[]{:S(2)}, u32[]{:S(2)}) async-start(f32[8,64,128]{2,1,0:T(8,128)} %broadcast_in_dim.5), calls=%async_computation.2 | async-start | bytes 524288 | tf_op jit(solution)/shard_map/all_to_all | solution.py:233
  144.5 36.7 %all-to-all-start.3 = ((f32[8,16,40,128]{3,2,1,0:T(8,128)}), f32[8,16,40,128]{3,2,1,0:T(8,128)S(1)}, u32[]{:S(2)}, u32[]{:S(2)}) async-start(f32[8,16,40,128]{3,2,1,0:T(8,128)} %image_copies.1), calls=%async_computation.3 | async-start | bytes 5242880 | tf_op jit(solution)/shard_map/all_to_all | solution.py:245

commit v5 on v4

--- a/solution.py
+++ b/solution.py
@@ -11,10 +11,34 @@
 HALVES = BAND // LANES
 TILE = 8
 PIECE = FINE * HALVES
-SLICE = BAND // 8 * HALVES
 FAR, NEAR, XS, YS, CORES = 16, 2, 4, 4, 2
 GROUPS = NEAR * XS
 COLS = YS * CORES
+EIGHTH = BAND // COLS
+KEPT = 5
+SLICE = EIGHTH * KEPT * EIGHTH // LANES
+AXES = ("far", "near", "x", "y", "core")
+
+
+def neighbours():
+    place = [
+        [
+            [far if near == 0 or core == 0 else (far - 1) % FAR, near, x, y, core]
+            for near in range(NEAR)
+            for x in range(XS)
+        ]
+        for far in range(FAR)
+        for y in range(YS)
+        for core in range(CORES)
+    ]
+
+    def index(at):
+        far, near, x, y, core = at
+        return (((far * NEAR + near) * XS + x) * YS + y) * CORES + core
+
+    return [[index(at) for at in group] for group in place]
+
+
 CHUNKS = 4
 NARROW = FAR // CHUNKS
 VMEM = pl.BlockSpec(memory_space=pltpu.VMEM)
@@ -63,6 +87,35 @@
         ],
         axis=1,
     )
+
+
+def turn(value, by):
+    return jnp.concatenate([value[:, by:], value[:, :by]], axis=1) if by else value
+
+
+def kept_blocks(matrix, c):
+    row = turn(matrix[c * EIGHTH : (c + 1) * EIGHTH, :], c * EIGHTH)
+    fold = LANES // EIGHTH
+    rest = row[:, LANES : KEPT * EIGHTH]
+    step = EIGHTH // fold
+    return jnp.concatenate(
+        [row[:, :LANES], jnp.concatenate([rest[i * step : (i + 1) * step, :] for i in range(fold)], axis=1)], axis=0
+    )
+
+
+def symmetric(ref, lo):
+    fold = LANES // EIGHTH
+    rows = []
+    for c in range(COLS):
+        rest = ref[c, lo + EIGHTH : lo + SLICE, :]
+        rest = jnp.concatenate([rest[:, i * EIGHTH : (i + 1) * EIGHTH] for i in range(fold)], axis=0)
+        empty = jnp.zeros((EIGHTH, BAND - KEPT * EIGHTH), jnp.float32)
+        row = jnp.concatenate([ref[c, lo : lo + EIGHTH, :], rest, empty], axis=1)
+        rows.append(turn(row, (BAND - c * EIGHTH) % BAND))
+    matrix = jnp.concatenate(rows, axis=0)
+    row_id = lax.broadcasted_iota(jnp.int32, (BAND, BAND), 0) // EIGHTH
+    col_id = lax.broadcasted_iota(jnp.int32, (BAND, BAND), 1) // EIGHTH
+    return jnp.where(lax.rem(col_id - row_id + COLS, COLS) < KEPT, matrix, matrix.T)
 
 
 def first_kernel(stored, gathered, panel, columns, payload, held, gone):
@@ -85,11 +138,10 @@
         odd += one_pass(turned_high, middle) + one_pass(turned_high, low)
     gram = even + (odd + odd.T)
     cross = precise(panel[...], image, ((0,), (0,)))
-    eighth = BAND // COLS
     for c in range(COLS):
         payload[c, :PIECE, :] = stack_halves(image[c * FINE : (c + 1) * FINE, :])
-        payload[c, PIECE : PIECE + SLICE, :] = stack_halves(gram[c * eighth : (c + 1) * eighth, :])
-        payload[c, PIECE + SLICE :, :] = stack_halves(cross[c * eighth : (c + 1) * eighth, :])
+        payload[c, PIECE : PIECE + SLICE, :] = kept_blocks(gram, c)
+        payload[c, PIECE + SLICE :, :] = kept_blocks(cross, c)
     for copy in outgoing:
         copy.wait()
 
@@ -143,10 +195,10 @@
             )
 
 
-def unstack(ref, lo, rows):
+def unstack(ref, rows):
     return jnp.concatenate(
         [
-            jnp.concatenate([ref[c, lo + h * rows : lo + (h + 1) * rows, :] for h in range(HALVES)], axis=1)
+            jnp.concatenate([ref[c, h * rows : (h + 1) * rows, :] for h in range(HALVES)], axis=1)
             for c in range(COLS)
         ],
         axis=0,
@@ -158,12 +210,12 @@
 
 
 def second_kernel(panel, small, left, right, work, scaled):
-    invert(unstack(small, PIECE, BAND // COLS), work, scaled)
+    invert(symmetric(small, PIECE), work, scaled)
     unit, over = work[:, BAND:], scaled[...]
     first = 2.0 * by_inverse(panel[...], unit, over)
     left[...] = first
-    own = unstack(small, 0, FINE)
-    cross = unstack(small, PIECE + SLICE, BAND // COLS)
+    own = unstack(small, FINE)
+    cross = symmetric(small, PIECE + SLICE)
     right[...] = 2.0 * by_inverse(own - precise(first, cross, ((1,), (0,))), unit, over)
 
 
@@ -192,8 +244,12 @@
     return pltpu.with_memory_space_constraint(value, pltpu.HBM)
 
 
-def copies(value, count):
-    return jnp.broadcast_to(value[None], (count, *value.shape))
+def copies(value):
+    return jnp.broadcast_to(value[None], (GROUPS, *value.shape))
+
+
+def exchange(value):
+    return lax.all_to_all(value, AXES, 0, 0, axis_index_groups=neighbours())
 
 
 def spread_kernel(far, out, gone):
@@ -209,13 +265,12 @@
     rows, width = stored.shape
     wide = width // CHUNKS
     col = ("y", "core")
-    group = ("near", "x")
     c = lax.axis_index(col)
     semaphores = pltpu.SemaphoreType.DMA((CHUNKS,))
     held = pltpu.VMEM((CHUNKS, BAND, wide), f32)
     tile = pltpu.VMEM((CHUNKS, rows, wide), f32)
     own = stack_halves(lax.dynamic_slice_in_dim(panel, c * FINE, FINE, 0))
-    gathered = lax.all_to_all(copies(lax.all_gather(own, "far", axis=0), GROUPS), group, 0, 0)
+    gathered = exchange(copies(lax.all_gather(own, "far", axis=0)))
     columns, payload = pl.pallas_call(
         first_kernel,
         out_shape=(
@@ -230,7 +285,7 @@
     )(stored, gathered, panel)
     summed = jnp.sum(lax.all_to_all(payload, col, 0, 0), axis=0)
     far = lax.all_gather(jnp.concatenate([summed[:PIECE], summed[PIECE + SLICE :]], axis=0), "far", axis=0)
-    parts = lax.all_to_all(copies(jnp.sum(far[:, PIECE:, :], axis=0), GROUPS), group, 0, 0)
+    parts = exchange(copies(jnp.sum(far[:, PIECE:, :], axis=0)))
     image = pl.pallas_call(
         spread_kernel,
         out_shape=pltpu.HBM((GROUPS, FAR, PIECE, LANES), f32),
@@ -242,7 +297,7 @@
         name="image_copies",
     )(far)
     image, parts = lax.optimization_barrier((image, parts))
-    image = lax.all_to_all(image, group, 0, 0)
+    image = exchange(image)
     small = lax.all_gather(
         jnp.concatenate([summed[: PIECE + SLICE], jnp.sum(parts, axis=0)], axis=0), col, axis=0
     )
@@ -269,7 +324,7 @@
 
 def solution(mesh):
     sizes = (FAR, NEAR, XS, YS, CORES)
-    fine_mesh = Mesh(mesh.devices.reshape(sizes), ("far", "near", "x", "y", "core"))
+    fine_mesh = Mesh(mesh.devices.reshape(sizes), AXES)
     row, col = ("far", "near", "x"), ("y", "core")
     return jax.shard_map(
         on_device, mesh=fine_mesh, in_specs=(P(row, col), P(row, None)), out_specs=P(row, col), check_vma=False

time: 186 us -> 189 us (1.016)
    all_gather x1, blocking collectives: 21.5 us -> 29.5 us  [on_device(): lax.all_gather(jnp.concatenate([summed[:PIECE + SLICE], jnp.sum(parts, ax...]
    all_to_all x1, blocking collectives: 25.5 us -> 20.8 us  [on_device(): summed = jnp.sum(lax.all_to_all(payload, col, 0, 0), axis=0)]
    all_gather x1, blocking collectives: 34.1 us -> 29.7 us  [on_device(): lax.all_gather(jnp.concatenate([summed[:PIECE], summed[PIECE + SLICE:]],...]
where the time goes in v5:
time: 189 us
  blocking collectives  152 us (80%)
  Pallas kernels  20.6 us (11%)
  starting transfers between devices  8.78 us (5%)
  waiting for transfers between devices  5.22 us (3%)
    all_gather x1, blocking collectives, on_device(): gathered = exchange(copies(lax.all_gather(own, 'far', axis=0)))  43 us
    all_gather x1, blocking collectives, on_device(): lax.all_gather(jnp.concatenate([summed[:PIECE], summed[PIECE + SLICE:]],...  29.7 us
    all_gather x1, blocking collectives, on_device(): lax.all_gather(jnp.concatenate([summed[:PIECE + SLICE], jnp.sum(parts, ax...  29.5 us
    all_to_all x1, blocking collectives, exchange(): return lax.all_to_all(value, AXES, 0, 0, axis_index_groups=neighbours())  29.3 us
    all_to_all x1, blocking collectives, on_device(): summed = jnp.sum(lax.all_to_all(payload, col, 0, 0), axis=0)  20.8 us
    pallas_call x1, Pallas kernels, on_device(): pl.pallas_call(second_kernel, out_shape=(jax.ShapeDtypeStruct((rows, BAND...  11.7 us
    all_to_all x2, starting transfers between devices, exchange(): return lax.all_to_all(value, AXES, 0, 0, axis_index_groups=neighbours())  8.78 us
    all_to_all x2, waiting for transfers between devices, exchange(): return lax.all_to_all(value, AXES, 0, 0, axis_index_groups=neighbours())  5.22 us
  transfers between devices with their start and end apart: 2, of which 1 were waited for; matrix products, arithmetic and copies ran while one was open for 0% of the time, Pallas kernels for 7%

profile of v5, /device:TPU:1, one launch (start us, length us, event | category | flops | bytes accessed | tf_op | source)
XLA Modules:
  0.0 188.9 jit_solution(10941474022681032437)
XLA Ops:
  0.0 0.8 constant_dynamic-slice_fusion
  0.8 43.0 %all-gather = f32[640,128]{1,0:T(8,128)S(1)} all-gather(f32[40,128]{1,0:T(8,128)S(1)} %pad_maximum_fusion.2), channel_id=2, replica_groups=mesh['far'=16,'near'=2,'x'=4,'y'=4,'core'=2] {'far'}, dimensions={0}, use_global_device_ids=true | all-gather | bytes 348160 | tf_op jit(solution)/shard_map/all_gather | solution.py:273
  43.8 0.2 broadcast_in_dim.4
  44.0 0.0 copy-start
  44.0 0.0 copy-start.1
  44.0 29.3 %all_to_all.20.gathered = f32[8,16,40,128]{3,2,1,0:T(8,128)S(1)} all-to-all(f32[8,16,40,128]{3,2,1,0:T(8,128)S(1)} %broadcast_in_dim.4), channel_id=1, replica_groups={{0,8,16,24,32,40,48,56},{1,9,17,25,993,1001,1009,1017},{2,10,18,26,34,4..., dimensions={0} | all-to-all | bytes 5242880 | tf_op jit(solution)/shard_map/all_to_all | solution.py:252
  73.3 0.0 copy-done
  73.4 0.0 copy-done.1
  73.4 3.2 %image_and_gram.1 = (f32[4,256,640]{2,1,0:T(8,128)}, f32[8,120,128]{2,1,0:T(8,128)S(1)}) custom-call(f32[160,2560]{1,0:T(8,128)S(1)} %copy-done, f32[8,16,40,128]{3,2,1,0:T(8,128)S(1)} %all_to_all.20.gathered, f32[160,256]{1,0:T(8,128)S(1)} %copy-done.1), custom_call_target="tpu_custom_call" | custom-call | tf_op jit(solution)/shard_map/image_and_gram/pallas_call | solution.py:274
  76.6 20.8 %all_to_all.21 = f32[8,120,128]{2,1,0:T(8,128)S(1)} all-to-all(f32[8,120,128]{2,1,0:T(8,128)S(1)} %get-tuple-element.11), channel_id=1, replica_groups=mesh['far'=16,'near'=2,'x'=4,'y'=4,'core'=2] {'y','core'}, dimensions={0} | all-to-all | bytes 983040 | tf_op jit(solution)/shard_map/all_to_all | solution.py:286
  97.5 29.7 %all-gather.1 = f32[1280,128]{1,0:T(8,128)S(1)} all-gather(f32[80,128]{1,0:T(8,128)S(1)} %pad_maximum_fusion.1), channel_id=3, replica_groups=mesh['far'=16,'near'=2,'x'=4,'y'=4,'core'=2] {'far'}, dimensions={0}, use_global_device_ids=true | all-gather | bytes 696320 | tf_op jit(solution)/shard_map/all_gather | solution.py:287
  127.2 0.7 broadcast_in_dim.5
  127.9 5.2 %all-to-all-start.2 = ((f32[8,40,128]{2,1,0:T(8,128)}), f32[8,40,128]{2,1,0:T(8,128)S(1)}, u32[]{:S(2)}, u32[]{:S(2)}) async-start(f32[8,40,128]{2,1,0:T(8,128)} %broadcast_in_dim.5), calls=%async_computation.2 | async-start | bytes 327680 | tf_op jit(solution)/shard_map/all_to_all | solution.py:252
  133.0 1.6 image_copies.1
  134.6 5.2 %all-to-all-done.2 = f32[8,40,128]{2,1,0:T(8,128)S(1)} async-done(((f32[8,40,128]{2,1,0:T(8,128)}), f32[8,40,128]{2,1,0:T(8,128)S(1)}, u32[]{:S(2)}, u32[]{:S(2)}) %all-to-all-start.2) | async-done | bytes 163872 | tf_op jit(solution)/shard_map/all_to_all | solution.py:252
  139.8 3.6 %all-to-all-start.3 = ((f32[8,16,40,128]{3,2,1,0:T(8,128)}), f32[8,16,40,128]{3,2,1,0:T(8,128)S(1)}, u32[]{:S(2)}, u32[]{:S(2)}) async-start(f32[8,16,40,128]{3,2,1,0:T(8,128)} %image_copies.1), calls=%async_computation.3 | async-start | bytes 5242880 | tf_op jit(solution)/shard_map/all_to_all | solution.py:252
  143.5 29.5 %all-gather.2 = f32[960,128]{1,0:T(8,128)S(1)} all-gather(f32[120,128]{1,0:T(8,128)S(1)} %pad_maximum_fusion), channel_id=4, replica_groups=mesh['far'=16,'near'=2,'x'=4,'y'=4,'core'=2] {'y','core'}, dimensions={0}, use_global_device_ids=true | all-gather | bytes 552960 | tf_op jit(solution)/shard_map/all_gather | solution.py:301
  173.0 11.7 %row_factors.1 = (f32[160,256]{1,0:T(8,128)S(1)}, f32[160,256]{1,0:T(8,128)S(1)}) custom-call(f32[160,256]{1,0:T(8,128)S(1)} %copy-done.1, f32[8,120,128]{2,1,0:T(8,128)S(1)} %bitcast.5), custom_call_target="tpu_custom_call" | custom-call | flops 10000000000 | bytes 2000000 | tf_op jit(solution)/shard_map/row_factors/pallas_call | solution.py:304
  184.7 0.0 all-to-all-done.3.pieces
  184.7 4.0 %update.1 = f32[160,2560]{1,0:T(8,128)} custom-call(f32[160,2560]{1,0:T(8,128)} %stored.3, f32[160,256]{1,0:T(8,128)S(1)} %get-tuple-element.13.left, f32[160,256]{1,0:T(8,128)S(1)} %get-tuple-element.14.right, f32[4,256,640]{2,1,0:T(8,128)} %get-tuple-element.15.columns, f32[8,16,40,128]{3,2,1,0:T(8,128)S(1)} %all-to-all-done.3.pieces), custom_call_target="tpu_custom_call" | custom-call | tf_op jit(solution)/shard_map/update/pallas_call | solution.py:314
  (8 shorter events, 0.1 us)
Async XLA Ops:
  44.0 29.3 %copy-start = (f32[160,2560]{1,0:T(8,128)S(1)}, f32[160,2560]{1,0:T(8,128)}, u32[]{:S(2)}) copy-start(f32[160,2560]{1,0:T(8,128)} %stored.3) | copy-start | bytes 4915204
  44.0 29.3 %copy-start.1 = (f32[160,256]{1,0:T(8,128)S(1)}, f32[160,256]{1,0:T(8,128)}, u32[]{:S(2)}) copy-start(f32[160,256]{1,0:T(8,128)} %panel.3) | copy-start | bytes 491524
  127.9 12.0 %all-to-all-start.2 = ((f32[8,40,128]{2,1,0:T(8,128)}), f32[8,40,128]{2,1,0:T(8,128)S(1)}, u32[]{:S(2)}, u32[]{:S(2)}) async-start(f32[8,40,128]{2,1,0:T(8,128)} %broadcast_in_dim.5), calls=%async_computation.2 | async-start | bytes 327680 | tf_op jit(solution)/shard_map/all_to_all | solution.py:252
  139.8 44.8 %all-to-all-start.3 = ((f32[8,16,40,128]{3,2,1,0:T(8,128)}), f32[8,16,40,128]{3,2,1,0:T(8,128)S(1)}, u32[]{:S(2)}, u32[]{:S(2)}) async-start(f32[8,16,40,128]{3,2,1,0:T(8,128)} %image_copies.1), calls=%async_computation.3 | async-start | bytes 5242880 | tf_op jit(solution)/shard_map/all_to_all | solution.py:252

commit v6 on v5

--- a/solution.py
+++ b/solution.py
@@ -18,27 +18,6 @@
 KEPT = 5
 SLICE = EIGHTH * KEPT * EIGHTH // LANES
 AXES = ("far", "near", "x", "y", "core")
-
-
-def neighbours():
-    place = [
-        [
-            [far if near == 0 or core == 0 else (far - 1) % FAR, near, x, y, core]
-            for near in range(NEAR)
-            for x in range(XS)
-        ]
-        for far in range(FAR)
-        for y in range(YS)
-        for core in range(CORES)
-    ]
-
-    def index(at):
-        far, near, x, y, core = at
-        return (((far * NEAR + near) * XS + x) * YS + y) * CORES + core
-
-    return [[index(at) for at in group] for group in place]
-
-
 CHUNKS = 4
 NARROW = FAR // CHUNKS
 VMEM = pl.BlockSpec(memory_space=pltpu.VMEM)
@@ -249,7 +228,7 @@
 
 
 def exchange(value):
-    return lax.all_to_all(value, AXES, 0, 0, axis_index_groups=neighbours())
+    return lax.all_to_all(value, ("near", "x"), 0, 0)
 
 
 def spread_kernel(far, out, gone):

time: 189 us -> 191 us (1.011)
  blocking collectives: 152 us -> 157 us
    all_gather x1, blocking collectives: 29.5 us -> 32.2 us  [on_device(): lax.all_gather(jnp.concatenate([summed[:PIECE + SLICE], jnp.sum(parts, ax...]
    all_to_all x1, blocking collectives: 20.8 us -> 23.3 us  [on_device(): summed = jnp.sum(lax.all_to_all(payload, col, 0, 0), axis=0)]
where the time goes in v6:
time: 191 us
  blocking collectives  157 us (82%)
  Pallas kernels  20.6 us (11%)
  starting transfers between devices  7.01 us (4%)
  waiting for transfers between devices  3.95 us (2%)
    all_gather x1, blocking collectives, on_device(): gathered = exchange(copies(lax.all_gather(own, 'far', axis=0)))  43 us
    all_gather x1, blocking collectives, on_device(): lax.all_gather(jnp.concatenate([summed[:PIECE + SLICE], jnp.sum(parts, ax...  32.2 us
    all_gather x1, blocking collectives, on_device(): lax.all_gather(jnp.concatenate([summed[:PIECE], summed[PIECE + SLICE:]],...  31.3 us
    all_to_all x1, blocking collectives, exchange(): return lax.all_to_all(value, ('near', 'x'), 0, 0)  27.5 us
    all_to_all x1, blocking collectives, on_device(): summed = jnp.sum(lax.all_to_all(payload, col, 0, 0), axis=0)  23.3 us
    pallas_call x1, Pallas kernels, on_device(): pl.pallas_call(second_kernel, out_shape=(jax.ShapeDtypeStruct((rows, BAND...  11.7 us
    all_to_all x2, starting transfers between devices, exchange(): return lax.all_to_all(value, ('near', 'x'), 0, 0)  7.01 us
    pallas_call x1, Pallas kernels, on_device(): pl.pallas_call(third_kernel, out_shape=jax.ShapeDtypeStruct((rows, width)...  4.05 us
  transfers between devices with their start and end apart: 2, of which 1 were waited for; matrix products, arithmetic and copies ran while one was open for 0% of the time, Pallas kernels for 7%

profile of v6, /device:TPU:1, one launch (start us, length us, event | category | flops | bytes accessed | tf_op | source)
XLA Modules:
  0.0 191.0 jit_solution(12505788835988553154)
XLA Ops:
  0.0 0.8 constant_dynamic-slice_fusion
  0.8 43.0 %all-gather = f32[640,128]{1,0:T(8,128)S(1)} all-gather(f32[40,128]{1,0:T(8,128)S(1)} %pad_maximum_fusion.2), channel_id=2, replica_groups=mesh['far'=16,'near'=2,'x'=4,'y'=4,'core'=2] {'far'}, dimensions={0}, use_global_device_ids=true | all-gather | bytes 348160 | tf_op jit(solution)/shard_map/all_gather | solution.py:252
  43.8 0.2 broadcast_in_dim.4
  44.0 0.0 copy-start
  44.0 0.0 copy-start.1
  44.0 27.5 %all_to_all.20.gathered = f32[8,16,40,128]{3,2,1,0:T(8,128)S(1)} all-to-all(f32[8,16,40,128]{3,2,1,0:T(8,128)S(1)} %broadcast_in_dim.4), channel_id=1, replica_groups=mesh['far'=16,'near'=2,'x'=4,'y'=4,'core'=2] {'near','x'}, dimensions={0} | all-to-all | bytes 5242880 | tf_op jit(solution)/shard_map/all_to_all | solution.py:231
  71.5 0.0 copy-done
  71.5 0.0 copy-done.1
  71.5 3.2 %image_and_gram.1 = (f32[4,256,640]{2,1,0:T(8,128)}, f32[8,120,128]{2,1,0:T(8,128)S(1)}) custom-call(f32[160,2560]{1,0:T(8,128)S(1)} %copy-done, f32[8,16,40,128]{3,2,1,0:T(8,128)S(1)} %all_to_all.20.gathered, f32[160,256]{1,0:T(8,128)S(1)} %copy-done.1), custom_call_target="tpu_custom_call" | custom-call | tf_op jit(solution)/shard_map/image_and_gram/pallas_call | solution.py:253
  74.8 23.3 %all_to_all.21 = f32[8,120,128]{2,1,0:T(8,128)S(1)} all-to-all(f32[8,120,128]{2,1,0:T(8,128)S(1)} %get-tuple-element.11), channel_id=1, replica_groups=mesh['far'=16,'near'=2,'x'=4,'y'=4,'core'=2] {'y','core'}, dimensions={0} | all-to-all | bytes 983040 | tf_op jit(solution)/shard_map/all_to_all | solution.py:265
  98.2 31.3 %all-gather.1 = f32[1280,128]{1,0:T(8,128)S(1)} all-gather(f32[80,128]{1,0:T(8,128)S(1)} %pad_maximum_fusion.1), channel_id=3, replica_groups=mesh['far'=16,'near'=2,'x'=4,'y'=4,'core'=2] {'far'}, dimensions={0}, use_global_device_ids=true | all-gather | bytes 696320 | tf_op jit(solution)/shard_map/all_gather | solution.py:266
  129.5 0.7 broadcast_in_dim.5
  130.2 3.4 %all-to-all-start.2 = ((f32[8,40,128]{2,1,0:T(8,128)}), f32[8,40,128]{2,1,0:T(8,128)S(1)}, u32[]{:S(2)}, u32[]{:S(2)}) async-start(f32[8,40,128]{2,1,0:T(8,128)} %broadcast_in_dim.5), calls=%async_computation.2 | async-start | bytes 327680 | tf_op jit(solution)/shard_map/all_to_all | solution.py:231
  133.6 1.6 image_copies.1
  135.2 3.9 %all-to-all-done.2 = f32[8,40,128]{2,1,0:T(8,128)S(1)} async-done(((f32[8,40,128]{2,1,0:T(8,128)}), f32[8,40,128]{2,1,0:T(8,128)S(1)}, u32[]{:S(2)}, u32[]{:S(2)}) %all-to-all-start.2) | async-done | bytes 163872 | tf_op jit(solution)/shard_map/all_to_all | solution.py:231
  139.2 3.6 %all-to-all-start.3 = ((f32[8,16,40,128]{3,2,1,0:T(8,128)}), f32[8,16,40,128]{3,2,1,0:T(8,128)S(1)}, u32[]{:S(2)}, u32[]{:S(2)}) async-start(f32[8,16,40,128]{3,2,1,0:T(8,128)} %image_copies.1), calls=%async_computation.3 | async-start | bytes 5242880 | tf_op jit(solution)/shard_map/all_to_all | solution.py:231
  142.8 32.2 %all-gather.2 = f32[960,128]{1,0:T(8,128)S(1)} all-gather(f32[120,128]{1,0:T(8,128)S(1)} %pad_maximum_fusion), channel_id=4, replica_groups=mesh['far'=16,'near'=2,'x'=4,'y'=4,'core'=2] {'y','core'}, dimensions={0}, use_global_device_ids=true | all-gather | bytes 552960 | tf_op jit(solution)/shard_map/all_gather | solution.py:280
  175.1 11.7 %row_factors.1 = (f32[160,256]{1,0:T(8,128)S(1)}, f32[160,256]{1,0:T(8,128)S(1)}) custom-call(f32[160,256]{1,0:T(8,128)S(1)} %copy-done.1, f32[8,120,128]{2,1,0:T(8,128)S(1)} %bitcast.5), custom_call_target="tpu_custom_call" | custom-call | flops 10000000000 | bytes 2000000 | tf_op jit(solution)/shard_map/row_factors/pallas_call | solution.py:283
  186.8 0.0 all-to-all-done.3.pieces
  186.8 4.0 %update.1 = f32[160,2560]{1,0:T(8,128)} custom-call(f32[160,2560]{1,0:T(8,128)} %stored.3, f32[160,256]{1,0:T(8,128)S(1)} %get-tuple-element.13.left, f32[160,256]{1,0:T(8,128)S(1)} %get-tuple-element.14.right, f32[4,256,640]{2,1,0:T(8,128)} %get-tuple-element.15.columns, f32[8,16,40,128]{3,2,1,0:T(8,128)S(1)} %all-to-all-done.3.pieces), custom_call_target="tpu_custom_call" | custom-call | tf_op jit(solution)/shard_map/update/pallas_call | solution.py:293
  (8 shorter events, 0.1 us)
Async XLA Ops:
  44.0 27.5 %copy-start = (f32[160,2560]{1,0:T(8,128)S(1)}, f32[160,2560]{1,0:T(8,128)}, u32[]{:S(2)}) copy-start(f32[160,2560]{1,0:T(8,128)} %stored.3) | copy-start | bytes 4915204
  44.0 27.5 %copy-start.1 = (f32[160,256]{1,0:T(8,128)S(1)}, f32[160,256]{1,0:T(8,128)}, u32[]{:S(2)}) copy-start(f32[160,256]{1,0:T(8,128)} %panel.3) | copy-start | bytes 491524
  130.2 8.9 %all-to-all-start.2 = ((f32[8,40,128]{2,1,0:T(8,128)}), f32[8,40,128]{2,1,0:T(8,128)S(1)}, u32[]{:S(2)}, u32[]{:S(2)}) async-start(f32[8,40,128]{2,1,0:T(8,128)} %broadcast_in_dim.5), calls=%async_computation.2 | async-start | bytes 327680 | tf_op jit(solution)/shard_map/all_to_all | solution.py:231
  139.2 47.6 %all-to-all-start.3 = ((f32[8,16,40,128]{3,2,1,0:T(8,128)}), f32[8,16,40,128]{3,2,1,0:T(8,128)S(1)}, u32[]{:S(2)}, u32[]{:S(2)}) async-start(f32[8,16,40,128]{3,2,1,0:T(8,128)} %image_copies.1), calls=%async_computation.3 | async-start | bytes 5242880 | tf_op jit(solution)/shard_map/all_to_all | solution.py:231

commit v7 on v6

--- a/solution.py
+++ b/solution.py
@@ -17,6 +17,7 @@
 EIGHTH = BAND // COLS
 KEPT = 5
 SLICE = EIGHTH * KEPT * EIGHTH // LANES
+SPARE = 24
 AXES = ("far", "near", "x", "y", "core")
 CHUNKS = 4
 NARROW = FAR // CHUNKS
@@ -263,8 +264,9 @@
         name="image_and_gram",
     )(stored, gathered, panel)
     summed = jnp.sum(lax.all_to_all(payload, col, 0, 0), axis=0)
-    far = lax.all_gather(jnp.concatenate([summed[:PIECE], summed[PIECE + SLICE :]], axis=0), "far", axis=0)
-    parts = exchange(copies(jnp.sum(far[:, PIECE:, :], axis=0)))
+    spare = jnp.zeros((SPARE, LANES), f32)
+    far = lax.all_gather(jnp.concatenate([summed[:PIECE], summed[PIECE + SLICE :], spare], axis=0), "far", axis=0)
+    parts = exchange(copies(jnp.sum(far[:, PIECE : PIECE + SLICE, :], axis=0)))
     image = pl.pallas_call(
         spread_kernel,
         out_shape=pltpu.HBM((GROUPS, FAR, PIECE, LANES), f32),

time: 191 us -> 184 us (0.963)
  blocking collectives: 157 us -> 125 us
  starting transfers between devices: 7.01 us -> 21.5 us
  waiting for transfers between devices: 3.95 us -> 13 us
    all_to_all x1 -> x0, blocking collectives: 23.3 us -> none  [on_device(): summed = jnp.sum(lax.all_to_all(payload, col, 0, 0), axis=0)]
    all_to_all x0 -> x1, starting transfers between devices: none -> 14.5 us  [on_device(): summed = jnp.sum(lax.all_to_all(payload, col, 0, 0), axis=0)]
    all_gather x1, blocking collectives: 32.2 us -> 20.8 us  [on_device(): lax.all_gather(jnp.concatenate([summed[:PIECE + SLICE], jnp.sum(parts, ax...]
    all_to_all x0 -> x1, waiting for transfers between devices: none -> 9.05 us  [on_device(): summed = jnp.sum(lax.all_to_all(payload, col, 0, 0), axis=0)]
    all_gather x1, blocking collectives: 31.3 us -> 34 us  [on_device(): lax.all_gather(jnp.concatenate([summed[:PIECE], summed[PIECE + SLICE:], s...]
  transfers between devices with their start and end apart: 2 -> 3, of which waited for: 1 -> 2; matrix products, arithmetic and copies ran while one was open for 0% -> 0% of each run, Pallas kernels for 7% -> 7%
where the time goes in v7:
time: 184 us; the launch traced here: 183 us
  blocking collectives  125 us (68%)
  starting transfers between devices  21.5 us (12%)
  Pallas kernels  21.3 us (12%)
  waiting for transfers between devices  13 us (7%)
    all_gather x1, blocking collectives, on_device(): gathered = exchange(copies(lax.all_gather(own, 'far', axis=0)))  43 us
    all_gather x1, blocking collectives, on_device(): lax.all_gather(jnp.concatenate([summed[:PIECE], summed[PIECE + SLICE:], s...  34 us
    all_to_all x1, blocking collectives, exchange(): return lax.all_to_all(value, ('near', 'x'), 0, 0)  27.5 us
    all_gather x1, blocking collectives, on_device(): lax.all_gather(jnp.concatenate([summed[:PIECE + SLICE], jnp.sum(parts, ax...  20.8 us
    all_to_all x1, starting transfers between devices, on_device(): summed = jnp.sum(lax.all_to_all(payload, col, 0, 0), axis=0)  14.5 us
    pallas_call x1, Pallas kernels, on_device(): pl.pallas_call(second_kernel, out_shape=(jax.ShapeDtypeStruct((rows, BAND...  11.7 us
    all_to_all x1, waiting for transfers between devices, on_device(): summed = jnp.sum(lax.all_to_all(payload, col, 0, 0), axis=0)  9.05 us
    all_to_all x2, starting transfers between devices, exchange(): return lax.all_to_all(value, ('near', 'x'), 0, 0)  7.01 us
  transfers between devices with their start and end apart: 3, of which 2 were waited for; matrix products, arithmetic and copies ran while one was open for 0% of the time, Pallas kernels for 7%

profile of v7, /device:TPU:1, one launch (start us, length us, event | category | flops | bytes accessed | tf_op | source)
XLA Modules:
  0.0 183.3 jit_solution(10118349587424168805)
XLA Ops:
  0.0 0.8 constant_dynamic-slice_fusion
  0.8 43.0 %all-gather = f32[640,128]{1,0:T(8,128)S(1)} all-gather(f32[40,128]{1,0:T(8,128)S(1)} %pad_maximum_fusion.1), channel_id=2, replica_groups=mesh['far'=16,'near'=2,'x'=4,'y'=4,'core'=2] {'far'}, dimensions={0}, use_global_device_ids=true | all-gather | bytes 348160 | tf_op jit(solution)/shard_map/all_gather | solution.py:253
  43.8 0.2 broadcast_in_dim.6
  44.0 0.0 copy-start
  44.0 0.0 copy-start.1
  44.0 27.5 %all_to_all.20.gathered = f32[8,16,40,128]{3,2,1,0:T(8,128)S(1)} all-to-all(f32[8,16,40,128]{3,2,1,0:T(8,128)S(1)} %broadcast_in_dim.6), channel_id=1, replica_groups=mesh['far'=16,'near'=2,'x'=4,'y'=4,'core'=2] {'near','x'}, dimensions={0} | all-to-all | bytes 5242880 | tf_op jit(solution)/shard_map/all_to_all | solution.py:232
  71.5 0.0 copy-done
  71.5 0.0 copy-done.1
  71.5 4.0 %image_and_gram.1 = (f32[4,256,640]{2,1,0:T(8,128)}, f32[8,120,128]{2,1,0:T(8,128)}) custom-call(f32[160,2560]{1,0:T(8,128)S(1)} %copy-done, f32[8,16,40,128]{3,2,1,0:T(8,128)S(1)} %all_to_all.20.gathered, f32[160,256]{1,0:T(8,128)S(1)} %copy-done.1), custom_call_target="tpu_custom_call" | custom-call | tf_op jit(solution)/shard_map/image_and_gram/pallas_call | solution.py:254
  75.5 14.5 %all-to-all-start.1 = ((f32[8,120,128]{2,1,0:T(8,128)}), f32[8,120,128]{2,1,0:T(8,128)S(1)}, u32[]{:S(2)}, u32[]{:S(2)}) async-start(f32[8,120,128]{2,1,0:T(8,128)} %get-tuple-element.11), calls=%async_computation.1 | async-start | bytes 983040 | tf_op jit(solution)/shard_map/all_to_all | solution.py:266
  90.0 0.1 pad.4.clone
  90.1 9.1 %all-to-all-done.1 = f32[8,120,128]{2,1,0:T(8,128)S(1)} async-done(((f32[8,120,128]{2,1,0:T(8,128)}), f32[8,120,128]{2,1,0:T(8,128)S(1)}, u32[]{:S(2)}, u32[]{:S(2)}) %all-to-all-start.1) | async-done | bytes 491552 | tf_op jit(solution)/shard_map/all_to_all | solution.py:266
  99.2 0.1 maximum_maximum_fusion
  99.2 34.0 %all-gather.1 = f32[1664,128]{1,0:T(8,128)S(1)} all-gather(f32[104,128]{1,0:T(8,128)S(1)} %maximum_maximum_fusion), channel_id=3, replica_groups=mesh['far'=16,'near'=2,'x'=4,'y'=4,'core'=2] {'far'}, dimensions={0}, use_global_device_ids=true | all-gather | bytes 905216 | tf_op jit(solution)/shard_map/all_gather | solution.py:268
  133.3 0.7 broadcast_in_dim.8
  133.9 3.4 %all-to-all-start.2 = ((f32[8,40,128]{2,1,0:T(8,128)}), f32[8,40,128]{2,1,0:T(8,128)S(1)}, u32[]{:S(2)}, u32[]{:S(2)}) async-start(f32[8,40,128]{2,1,0:T(8,128)} %broadcast_in_dim.8), calls=%async_computation.2 | async-start | bytes 327680 | tf_op jit(solution)/shard_map/all_to_all | solution.py:232
  137.3 1.6 image_copies.1
  138.9 4.0 %all-to-all-done.2 = f32[8,40,128]{2,1,0:T(8,128)S(1)} async-done(((f32[8,40,128]{2,1,0:T(8,128)}), f32[8,40,128]{2,1,0:T(8,128)S(1)}, u32[]{:S(2)}, u32[]{:S(2)}) %all-to-all-start.2) | async-done | bytes 163872 | tf_op jit(solution)/shard_map/all_to_all | solution.py:232
  142.9 3.6 %all-to-all-start.3 = ((f32[8,16,40,128]{3,2,1,0:T(8,128)}), f32[8,16,40,128]{3,2,1,0:T(8,128)S(1)}, u32[]{:S(2)}, u32[]{:S(2)}) async-start(f32[8,16,40,128]{3,2,1,0:T(8,128)} %image_copies.1), calls=%async_computation.3 | async-start | bytes 5242880 | tf_op jit(solution)/shard_map/all_to_all | solution.py:232
  146.6 20.8 %all-gather.2 = f32[960,128]{1,0:T(8,128)S(1)} all-gather(f32[120,128]{1,0:T(8,128)S(1)} %pad_maximum_fusion), channel_id=4, replica_groups=mesh['far'=16,'near'=2,'x'=4,'y'=4,'core'=2] {'y','core'}, dimensions={0}, use_global_device_ids=true | all-gather | bytes 552960 | tf_op jit(solution)/shard_map/all_gather | solution.py:282
  167.4 11.7 %row_factors.1 = (f32[160,256]{1,0:T(8,128)S(1)}, f32[160,256]{1,0:T(8,128)S(1)}) custom-call(f32[160,256]{1,0:T(8,128)S(1)} %copy-done.1, f32[8,120,128]{2,1,0:T(8,128)S(1)} %bitcast.5), custom_call_target="tpu_custom_call" | custom-call | flops 10000000000 | bytes 2000000 | tf_op jit(solution)/shard_map/row_factors/pallas_call | solution.py:285
  179.0 0.0 all-to-all-done.3.pieces
  179.0 4.0 %update.1 = f32[160,2560]{1,0:T(8,128)} custom-call(f32[160,2560]{1,0:T(8,128)} %stored.3, f32[160,256]{1,0:T(8,128)S(1)} %get-tuple-element.13.left, f32[160,256]{1,0:T(8,128)S(1)} %get-tuple-element.14.right, f32[4,256,640]{2,1,0:T(8,128)} %get-tuple-element.15.columns, f32[8,16,40,128]{3,2,1,0:T(8,128)S(1)} %all-to-all-done.3.pieces), custom_call_target="tpu_custom_call" | custom-call | tf_op jit(solution)/shard_map/update/pallas_call | solution.py:295
  (8 shorter events, 0.1 us)
Async XLA Ops:
  44.0 27.5 %copy-start = (f32[160,2560]{1,0:T(8,128)S(1)}, f32[160,2560]{1,0:T(8,128)}, u32[]{:S(2)}) copy-start(f32[160,2560]{1,0:T(8,128)} %stored.3) | copy-start | bytes 4915204
  44.0 27.5 %copy-start.1 = (f32[160,256]{1,0:T(8,128)S(1)}, f32[160,256]{1,0:T(8,128)}, u32[]{:S(2)}) copy-start(f32[160,256]{1,0:T(8,128)} %panel.3) | copy-start | bytes 491524
  75.5 23.6 %all-to-all-start.1 = ((f32[8,120,128]{2,1,0:T(8,128)}), f32[8,120,128]{2,1,0:T(8,128)S(1)}, u32[]{:S(2)}, u32[]{:S(2)}) async-start(f32[8,120,128]{2,1,0:T(8,128)} %get-tuple-element.11), calls=%async_computation.1 | async-start | bytes 983040 | tf_op jit(solution)/shard_map/all_to_all | solution.py:266
  133.9 8.9 %all-to-all-start.2 = ((f32[8,40,128]{2,1,0:T(8,128)}), f32[8,40,128]{2,1,0:T(8,128)S(1)}, u32[]{:S(2)}, u32[]{:S(2)}) async-start(f32[8,40,128]{2,1,0:T(8,128)} %broadcast_in_dim.8), calls=%async_computation.2 | async-start | bytes 327680 | tf_op jit(solution)/shard_map/all_to_all | solution.py:232
  142.9 36.2 %all-to-all-start.3 = ((f32[8,16,40,128]{3,2,1,0:T(8,128)}), f32[8,16,40,128]{3,2,1,0:T(8,128)S(1)}, u32[]{:S(2)}, u32[]{:S(2)}) async-start(f32[8,16,40,128]{3,2,1,0:T(8,128)} %image_copies.1), calls=%async_computation.3 | async-start | bytes 5242880 | tf_op jit(solution)/shard_map/all_to_all | solution.py:232
